TPU v7x, 128 devices: a whole 4x4x4 slice. The times are simulated.
128 devices in a mesh: seq: 64 (over x, y, z), head: 2 (over core).
Axes of the slice: x: 4, y: 4, z: 4, core: 2. Of those that a mesh axis runs over, the one named last changes fastest.
Arguments:
- queries: bfloat16 [65536, 2048], P(('seq', 'head')), may hold values from -120 to 120
- keys: bfloat16 [65536, 2048], P(('seq', 'head')), may hold values from -4.5 to 4.5
- values: bfloat16 [65536, 2048], P(('seq', 'head')), may hold values from -6 to 6
- offsets: int32 [2, 4], replicated, may hold values from 0 to 31, as said below
Outputs:
- attention_out: bfloat16 [65536, 2048], P(('seq', 'head'))
Inputs may be any that keep to these rules, and one draw needn't show every extreme that they name: offsets[0, g] is below 2 and offsets[1, g] is below 32; some head group has offsets[0, g] = 0 and some head group has offsets[1, g] = 31.
All inputs are finite; a program needn't handle non-finite values.
Results may differ from a plain program's by a relative error of at most 0.0032.
Values may be sent and summed in bfloat16 or wider, within the bound.
No kernel may reach another device: no remote copies, remote signals or barrier semaphores. Data moves between devices by JAX's collectives and lax.ppermute only.
A program may use at most 128 MiB of HBM per device.

v0:
```python
import functools

import jax
import jax.numpy as jnp
import numpy as np
from jax import lax
from jax.experimental import pallas as pl
from jax.experimental.pallas import tpu as pltpu
from jax.sharding import Mesh
from jax.sharding import PartitionSpec as P

HD = 128
BLK = 128
HALF = 64
HEADS = 16
GROUPS = 4
GH = 4
GW = GH * HD
ROWS = 512
NSEL = 256
AXES = ("x", "y", "z", "c")
SIZES = (4, 4, 4, 2)
SCALE = float(HD**-0.5 * np.log2(np.e))
LOW = -1e30
BF, F32 = jnp.bfloat16, jnp.float32


class Place:
    def __init__(self, offsets):
        self.x, self.y, self.z, self.core = (lax.axis_index(a) for a in AXES)
        self.offsets = offsets
        self.odd = self.z % 2 == 1

    def near(self, g):
        return self.offsets[0, g]

    def far_z(self, g):
        return self.offsets[1, g] // 8

    def far_core(self, g):
        return self.offsets[1, g] // 4 % 2

    def far_block(self, g):
        return self.offsets[1, g] % 4

    def far_here(self, g):
        return (self.far_z(g) == self.z) & (self.far_core(g) == self.core)


def route(step):
    pairs = []
    for index in np.ndindex(*SIZES):
        target = step(*index)
        if target is not None:
            pairs.append((int(np.ravel_multi_index(index, SIZES)), int(np.ravel_multi_index(target, SIZES))))
    return pairs


CORE = route(lambda x, y, z, c: (x, y, z, 1 - c))
PAIR = route(lambda x, y, z, c: (x, y, z ^ 1, c))
TO_ODD = route(lambda x, y, z, c: (x, y, z + 1, c) if z % 2 == 0 else None)


def move(array, pairs):
    return lax.ppermute(array, AXES, pairs)


def cost(flops=1000):
    return pl.CostEstimate(flops=flops, bytes_accessed=1000, transcendentals=0)


ANY = pl.BlockSpec(memory_space=pl.ANY)
SMEM = pl.BlockSpec(memory_space=pltpu.SMEM)
PARAMS = dict(vmem_limit_bytes=28 * 1024 * 1024)


def nt(a, b):
    return lax.dot_general(a, b, (((1,), (1,)), ((), ())), preferred_element_type=F32)


def nn(a, b):
    return lax.dot_general(a, b, (((1,), (0,)), ((), ())), preferred_element_type=F32)


def three(x):
    hi = x.astype(BF).astype(F32)
    rest = x - hi
    mid = rest.astype(BF).astype(F32)
    return hi, mid, rest - mid


def in_three(stats, lane, heads):
    hi, mid, low = three(stats)
    return jnp.where(lane < heads, hi, jnp.where(lane < 2 * heads, mid, low)).astype(BF)


def rows_at(first, count):
    return pl.ds(pl.multiple_of(first, count), count)


def group_cols(g):
    return pl.ds(g * GW, GW)


def run_copies(copies):
    for c in copies:
        c.start()
    for c in copies:
        c.wait()


def pack_first(offsets, q, k, v, near, send, keep, sems):
    here = Place(offsets)
    copies = []
    for g in range(GROUPS):
        for t, source in enumerate((q, k, v)):
            first = here.far_block(g) * BLK
            for half, target in ((1 - here.core, send), (here.core, keep)):
                rows = rows_at(first + half * HALF, HALF)
                copies.append(
                    pltpu.make_async_copy(source.at[rows, group_cols(g)], target.at[g, t], sems.at[len(copies)])
                )
    for odd in (False, True):

        @pl.when(here.odd == odd)
        def _():
            nears = []
            for g in range(2):
                for half in range(2):
                    rows = rows_at((here.near(g if odd else g + 2) + 2 * half) * BLK, BLK)
                    to = pl.ds(half * BLK, BLK)
                    for t, source in enumerate((q,) if odd else (k, v)):
                        nears.append(
                            pltpu.make_async_copy(
                                source.at[rows, group_cols(g if odd else g + 2)],
                                near.at[t, to, group_cols(g)],
                                sems.at[len(copies) + len(nears)],
                            )
                        )
            run_copies(copies + nears)


def pack_second(offsets, kept, received, out):
    here = Place(offsets)
    for g in range(GROUPS):
        mine = here.far_core(g) == here.core
        for source, flag in ((kept, mine), (received, jnp.logical_not(mine))):

            @pl.when(flag)
            def _():
                for t in range(3):
                    for h in range(GH):
                        out[h * GROUPS + g, t] = source[g, t, :, h * HD : (h + 1) * HD]


def with_ones(val):
    return jnp.concatenate([val, jnp.ones((val.shape[0], HD), BF)], axis=1)


def with_ones(val):
    return jnp.concatenate([val, jnp.ones((val.shape[0], HD), BF)], axis=1)


def softmax_parts(parts, values):
    top = functools.reduce(jnp.maximum, [jnp.max(s, axis=1, keepdims=True) for s in parts]) * SCALE
    both = 0.0
    for s, val in zip(parts, values):
        both = both + nn(jnp.exp2(s * SCALE - top).astype(BF), with_ones(val))
    return both[:, :HD] / both[:, HD:], top + jnp.log2(both[:, HD:])


def head_cols(h):
    return slice(h * HD, (h + 1) * HD)


def near_part(heads, q_of, keys_of, vals_of, out):
    lane = lax.broadcasted_iota(jnp.int32, (NSEL, HD), 1)
    stats = jnp.zeros((NSEL, HD), F32)
    for h in range(heads):
        keys = jnp.concatenate(keys_of(h), axis=0)
        vals = jnp.concatenate(vals_of(h), axis=0)
        o, m = softmax_parts([nt(q_of(h), keys)], [vals])
        out[:, head_cols(h)] = o.astype(BF)
        stats = jnp.where(lane % heads == h, m, stats)
    out[:, heads * HD :] = in_three(stats, lane, heads)


def near_even(offsets, qr, k, ko, v, vo, out, keys, vals, sems):
    here = Place(offsets)

    @pl.when(jnp.logical_not(here.odd))
    def _():
        copies = []
        for g in range(2):
            for n, (source, half) in enumerate([(0, 0), (0, 1), (1, 0), (1, 1)]):
                rows = rows_at((here.near(g) + 2 * half) * BLK, BLK)
                for two, target in (((k, ko), keys), ((v, vo), vals)):
                    copies.append(
                        pltpu.make_async_copy(
                            two[source].at[rows, group_cols(g)],
                            target.at[pl.ds(n * BLK, BLK), group_cols(g)],
                            sems.at[len(copies)],
                        )
                    )
        run_copies(copies)
        near_part(
            2 * GH,
            lambda h: qr[0, :, head_cols(h)],
            lambda h: [keys[:, head_cols(h)]],
            lambda h: [vals[:, head_cols(h)]],
            out,
        )


def far_kernel(offsets, mine, other, out):
    here = Place(offsets)

    @pl.when(here.far_z(here.y) == here.z)
    def _():
        late = here.core == 1
        for t in range(4):
            upto = 4 * t + 4
            q = mine[4 * t : upto, 0].reshape(256, HD)
            ri = lax.broadcasted_iota(jnp.int32, (256, 256), 0)
            ci = lax.broadcasted_iota(jnp.int32, (256, 256), 1)
            own_ok = (ci // HALF < ri // HALF) | ((ci // HALF == ri // HALF) & (ci <= ri))
            oth_ok = (ci // HALF < ri // HALF) | ((ci // HALF == ri // HALF) & late)
            parts, vals = [], []
            for source, ok in ((mine, own_ok), (other, oth_ok)):
                s = nt(q, source[0:upto, 1].reshape(upto * HALF, HD))
                d = jnp.where(ok, s[:, t * 256 :], LOW)
                parts.append(d if t == 0 else jnp.concatenate([s[:, : t * 256], d], axis=1))
                vals.append(source[0:upto, 2].reshape(upto * HALF, HD))
            o, m = softmax_parts(parts, vals)
            o = o.astype(BF)
            turned = jnp.transpose(m)[0:16]
            row = lax.broadcasted_iota(jnp.int32, (16, 256), 0)
            stats = jnp.zeros((16, 256), F32)
            for n, term in enumerate(three(turned)):
                stats = jnp.where(row == n, term, stats)
            stats = stats.astype(BF)
            for b in range(4):
                out[4 * t + b, 0:HALF] = o[b * HALF : (b + 1) * HALF]
                out[4 * t + b, HALF:] = stats[:, (b // 2) * 128 : (b // 2) * 128 + 128]


def spread_lanes(stats, places):
    line = lax.broadcasted_iota(jnp.int32, (HD, HD), 0)
    hit = functools.reduce(jnp.logical_or, [line == p for p in places])
    return nn(stats, jnp.where(hit, 1.0, 0.0).astype(BF))


def far_piece(here, far_own, far_oth, g, h):
    outs, masses = [], []
    picks = lax.broadcasted_iota(jnp.int32, (16, HD), 0) < 3
    picks = jnp.where(picks, 1.0, 0.0).astype(BF)
    for source in (far_own, far_oth):
        tile = source[h * GROUPS + g]
        outs.append(tile[0:HALF].astype(F32))
        turned = lax.dot_general(
            tile[HALF:], picks, (((0,), (0,)), ((), ())), preferred_element_type=F32
        )
        masses.append(jnp.where(here.y % 2 == 1, turned[HALF:], turned[:HALF]))
    first = here.core == 0

    def ordered(a, b):
        return jnp.concatenate([jnp.where(first, a, b), jnp.where(first, b, a)], axis=0)

    return ordered(*outs), ordered(*masses)


def local_parts(core):
    if core == 0:
        return [[("own", 256, True)], [("own", 512, False), ("oth", 512, True)]]
    return [[("oth", 512, False), ("own", 256, True)], [("oth", 512, True)]]


def local_weights(near, parts, scores):
    extra = [jnp.where(near == i, 1.0, 0.0).astype(F32) for i in range(2)]
    causal = lax.broadcasted_iota(jnp.int32, (BLK, BLK), 0) >= lax.broadcasted_iota(jnp.int32, (BLK, BLK), 1)
    weights, tops = [[] for _ in scores], []
    for i in range(2):
        blocks = []
        for (_, count, diagonal), sc in zip(parts, scores):
            upto = count // BLK - (1 - i if diagonal else 0)
            mine = [sc[i * BLK : (i + 1) * BLK, j * BLK : (j + 1) * BLK] for j in range(upto)]
            if diagonal:
                mine[-1] = jnp.where(causal, mine[-1], LOW)
            blocks.append(mine)
        top = functools.reduce(jnp.maximum, sum(blocks, []))
        top = jnp.max(top, axis=1, keepdims=True) * SCALE
        raised = top - extra[i]
        for n, mine in enumerate(blocks):
            pieces = [
                jnp.exp2(b * SCALE - (raised if j % 2 == i else top)).astype(BF) for j, b in enumerate(mine)
            ]
            pieces += [jnp.zeros((BLK, BLK), BF)] * (parts[n][1] // BLK - len(pieces))
            weights[n].append(jnp.concatenate(pieces, axis=1))
        tops.append(jnp.broadcast_to(top, (BLK, HD)))
    return [jnp.concatenate(w, axis=0) for w in weights], jnp.concatenate(tops, axis=0)


UNROLL = GH


def local_kernel(offsets, q_in, qo_in, k_in, ko_in, v_in, vo_in, mine, away, q, qo, k, ko, v, vo, stats, sems):
    here = Place(offsets)
    keys, vals = {"own": k, "oth": ko}, {"own": v, "oth": vo}
    lane = lax.broadcasted_iota(jnp.int32, (NSEL, HD), 1)
    stats[...] = jnp.zeros_like(stats)

    for core in range(2):
        tiles = local_parts(core)
        own = 512 if core == 0 else 256

        def stage(g, own=own):
            cols = pl.ds(pl.multiple_of(g * GW, GW), GW)
            pieces = (
                (q_in, 0, q, 256),
                (k_in, 0, k, own),
                (ko_in, 0, ko, 512),
                (qo_in, 256, qo, 256),
                (v_in, 0, v, own),
                (vo_in, 0, vo, 512),
            )
            return [
                pltpu.make_async_copy(a.at[pl.ds(first, n), cols], b.at[pl.ds(0, n), cols], sems.at[g, i])
                for i, (a, first, b, n) in enumerate(pieces)
            ]

        @pl.when(here.core == core)
        def _():
            for g in range(GROUPS):
                for c in stage(g):
                    c.start()

            @pl.loop(0, HEADS // UNROLL)
            def _(turn):
                for c in stage(turn):
                    c.wait()
                items = [(h, t) for h in range(UNROLL) for t in range(2)]

                def cols(h):
                    return pl.ds(pl.multiple_of(turn * (UNROLL * HD), HD) + h * HD, HD)

                def score(h, t):
                    queries = (qo if t else q)[:, cols(h)]
                    return [nt(queries, keys[w][0:n, cols(h)]) for w, n, _ in tiles[t]]

                def finish(h, t, weights, top):
                    target = (mine, away)[t]
                    both = 0.0
                    for (w, n, _), p in zip(tiles[t], weights):
                        both = both + nn(p, with_ones(vals[w][0:n, cols(h)]))
                    target[:, cols(h)] = (both[:, :HD] / both[:, HD:]).astype(BF)
                    here_lane = lane % HEADS == turn * UNROLL + h
                    stats[t] = jnp.where(here_lane, top + jnp.log2(both[:, HD:]), stats[t])

                scores = score(*items[0])
                last = None
                for n, (h, t) in enumerate(items):
                    ahead = score(*items[n + 1]) if n + 1 < len(items) else None
                    current = local_weights(here.near((turn * UNROLL + h) // GH), tiles[t], scores)
                    if last is not None:
                        finish(*last)
                    last = (h, t, *current)
                    scores = ahead
                finish(*last)

    for t, target in enumerate((mine, away)):
        target[:, HEADS * HD :] = in_three(stats[t], lane, HEADS)


def mix(parts):
    top = functools.reduce(jnp.maximum, [m for _, m in parts])
    up = down = 0.0
    for o, m in parts:
        e = jnp.exp2(m - top)
        up, down = up + e * o, down + e
    return (up / down).astype(BF)


def own_part(halves, half, rows, g, h):
    source = halves[half]
    return (
        source[rows, pl.ds(g * GW + h * HD, HD)].astype(F32),
        spread_lanes(source[rows, HEADS * HD :], [n * HEADS + g * GH + h for n in range(3)]),
    )


def next_part(nears, half, g, h):
    rows = slice(half * BLK, (half + 1) * BLK)
    source, place = nears[g // 2], (g % 2) * GH + h
    return (
        source[rows, head_cols(place)].astype(F32),
        spread_lanes(source[rows, 2 * GW :], [n * 2 * GH + place for n in range(3)]),
    )


def settle(offsets, q, kv_a, kv_b, mine, back, out, near, queries, done, sems, out_sems):
    here = Place(offsets)
    halves = (mine, back)
    copies = []
    for g in range(2):
        for half in range(2):
            rows = rows_at((here.near(2 + g) + 2 * half) * BLK, BLK)
            copies.append(
                pltpu.make_async_copy(
                    q.at[rows, group_cols(2 + g)],
                    queries.at[pl.ds(half * BLK, BLK), group_cols(g)],
                    sems.at[len(copies)],
                )
            )

    @pl.when(here.odd)
    def _():
        for c in copies:
            c.start()

    for half in range(2):
        done[half * NSEL : (half + 1) * NSEL, :] = halves[half][:, : HEADS * HD]

    def leave(g):
        return pltpu.make_async_copy(done.at[:, group_cols(g)], out.at[:, group_cols(g)], out_sems.at[g])

    leave(0).start()
    leave(1).start()

    @pl.when(here.odd)
    def _():
        for c in copies:
            c.wait()
        near_part(
            2 * GH,
            lambda h: queries[:, head_cols(h)],
            lambda h: [r[0, :, head_cols(h)] for r in (kv_a, kv_b)],
            lambda h: [r[1, :, head_cols(h)] for r in (kv_a, kv_b)],
            near,
        )
        for g in (2, 3):
            rows = rows_at(here.near(g) * BLK, BLK)
            for half in range(2):
                to = rows_at(here.near(g) * BLK + half * NSEL, BLK)
                for h in range(GH):
                    parts = [own_part(halves, half, rows, g, h), next_part((None, near), half, g, h)]
                    done[to, pl.ds(g * GW + h * HD, HD)] = mix(parts)

    leave(2).start()
    leave(3).start()
    for g in range(GROUPS):
        leave(g).wait()


def finish_kernel(
    offsets, mine, back, near_a, far_own, far_oth, near_in, before, out, near_o, far_o, near_b, near_sems, far_sems, sem
):
    here = Place(offsets)
    nears, halves = (near_a, near_b), (mine, back)
    want_near_b = here.odd & (here.far_here(2) | here.far_here(3))
    fetch = pltpu.make_async_copy(near_in, near_b, sem)

    @pl.when(want_near_b)
    def _():
        fetch.start()

    def near_copy(g, half):
        rows = rows_at((here.near(g) + 2 * half) * BLK, BLK)
        return pltpu.make_async_copy(near_o.at[g, half], out.at[rows, group_cols(g)], near_sems.at[g, half])

    def far_copy(g):
        rows = rows_at(here.far_block(g) * BLK, BLK)
        return pltpu.make_async_copy(far_o.at[g], out.at[rows, group_cols(g)], far_sems.at[g])

    def near_here(g, half):
        return here.odd & jnp.logical_not(here.far_here(g) & (here.far_block(g) == here.near(g) + 2 * half))

    for g in range(2):
        rows = rows_at(here.near(g) * BLK, BLK)
        for half in range(2):

            @pl.when(near_here(g, half))
            def _():
                for h in range(GH):
                    parts = [own_part(halves, half, rows, g, h), next_part(nears, half, g, h)]
                    near_o[g, half, :, head_cols(h)] = mix(parts)
                near_copy(g, half).start()

    @pl.when(want_near_b)
    def _():
        fetch.wait()

    for g in range(GROUPS):
        rows = rows_at(here.far_block(g) % 2 * BLK, BLK)
        near_too = here.odd & (here.far_block(g) % 2 == here.near(g))
        for half in range(2):
            for both in (False, True):

                @pl.when(here.far_here(g) & (here.far_block(g) // 2 == half) & (near_too == both))
                def _():
                    for h in range(GH):
                        parts = [own_part(halves, half, rows, g, h), far_piece(here, far_own, far_oth, g, h)]
                        if both:
                            parts.append(next_part(nears, half, g, h))
                        far_o[g, :, head_cols(h)] = mix(parts)
                    far_copy(g).start()

    for g in range(GROUPS):

        @pl.when(here.far_here(g))
        def _():
            far_copy(g).wait()

    for g in range(2):
        for half in range(2):

            @pl.when(near_here(g, half))
            def _():
                near_copy(g, half).wait()


VMEM = pl.BlockSpec(memory_space=pltpu.VMEM)
HBM = pl.BlockSpec(memory_space=pltpu.HBM)


def shape(*dims):
    return jax.ShapeDtypeStruct(dims, BF)


def hbm(array):
    return pltpu.with_memory_space_constraint(array, pltpu.HBM)


def device_part(q, k, v, offsets):
    params = pltpu.CompilerParams(**PARAMS)

    def call(kernel, outs, operands, places, sems=None, scratch=(), out_places=VMEM, flops=1000, aliases=None):
        return pl.pallas_call(
            kernel,
            out_shape=outs,
            in_specs=[SMEM] + places,
            out_specs=out_places,
            scratch_shapes=list(scratch) + ([] if sems is None else [pltpu.SemaphoreType.DMA((sems,))]),
            input_output_aliases=aliases or {},
            compiler_params=params,
            cost_estimate=cost(flops),
            name=kernel.__name__,
        )(hbm(offsets), *operands)

    qh, kh, vh = hbm(q), hbm(k), hbm(v)
    half_shape = shape(GROUPS, 3, HALF, GW)
    near_x, far_send, far_keep = call(
        pack_first,
        [pltpu.VMEM((2, NSEL, 2 * GW), BF), half_shape, half_shape],
        (qh, kh, vh),
        [HBM] * 3,
        sems=6 * GROUPS + 8,
        out_places=[VMEM] * 3,
    )
    far_recv = move(far_send, CORE)
    near_r = move(near_x, PAIR)
    qm, far_recv = lax.optimization_barrier((q, far_recv))
    qo, ko, vo = hbm(move(qm, CORE)), hbm(move(k, CORE)), hbm(move(v, CORE))
    far_pack = call(pack_second, shape(HEADS, 3, HALF, HD), (far_keep, far_recv), [VMEM] * 2)
    far_mine = lax.all_to_all(far_pack, ("x", "y"), 0, 0, tiled=True)

    rows = HEADS * HD
    mine, away = call(
        local_kernel,
        [shape(NSEL, rows + HD), pltpu.HBM((NSEL, rows + HD), BF)],
        (qh, qo, kh, ko, vh, vo),
        [HBM] * 6,
        scratch=[pltpu.VMEM((n, rows), BF) for n in (NSEL, NSEL, ROWS, ROWS, ROWS, ROWS)]
        + [pltpu.VMEM((2, NSEL, HD), F32), pltpu.SemaphoreType.DMA((GROUPS, 6))],
        out_places=[VMEM] * 2,
        flops=10**10,
    )
    back = move(away, CORE)
    far_mine, mine = lax.optimization_barrier((far_mine, mine))
    far_other = move(far_mine, CORE)
    far_out = call(far_kernel, pltpu.HBM((HEADS, HALF + 16, HD), BF), (far_mine, far_other), [VMEM] * 2)
    near_r, far_out = lax.optimization_barrier((near_r, far_out))
    near_ro = move(near_r, CORE)
    near_out = call(
        near_even,
        shape(NSEL, 2 * GW + HD),
        (near_r, kh, ko, vh, vo),
        [VMEM] + [HBM] * 4,
        sems=16,
        scratch=[pltpu.VMEM((ROWS, 2 * GW), BF)] * 2,
    )
    near_back = move(near_out, TO_ODD)
    far_out, near_out = lax.optimization_barrier((far_out, near_out))
    far_back = lax.all_to_all(far_out, ("x", "y"), 0, 0, tiled=True)
    out, near_here = call(
        settle,
        [shape(ROWS, HEADS * HD), pltpu.HBM((NSEL, 2 * GW + HD), BF)],
        (qh, near_r, near_ro, mine, back),
        [HBM] + [VMEM] * 4,
        scratch=[
            pltpu.VMEM((NSEL, 2 * GW), BF),
            pltpu.VMEM((ROWS, HEADS * HD), BF),
            pltpu.SemaphoreType.DMA((4,)),
            pltpu.SemaphoreType.DMA((GROUPS,)),
        ],
        out_places=[HBM, VMEM],
    )
    near_here = hbm(near_here)
    far_back, near_back, out = lax.optimization_barrier((far_back, near_back, out))
    far_back_other = move(far_back, CORE)
    return call(
        finish_kernel,
        shape(ROWS, HEADS * HD),
        (mine, back, near_back, far_back, far_back_other, near_here, out),
        [VMEM] * 5 + [HBM] * 2,
        scratch=[
            pltpu.VMEM((2, 2, BLK, GW), BF),
            pltpu.VMEM((GROUPS, BLK, GW), BF),
            pltpu.VMEM((NSEL, 2 * GW + HD), BF),
            pltpu.SemaphoreType.DMA((2, 2)),
            pltpu.SemaphoreType.DMA((GROUPS,)),
            pltpu.SemaphoreType.DMA,
        ],
        out_places=HBM,
        aliases={7: 0},
    )


def solution(mesh):
    cube = Mesh(mesh.devices.reshape(SIZES), AXES)
    rows = P(AXES, None)
    return jax.shard_map(
        device_part, mesh=cube, in_specs=(rows, rows, rows, P()), out_specs=rows, check_vma=False
    )
```

profile of v0, /device:TPU:65, one launch (start us, length us, event | category | flops | bytes accessed | tf_op | source)
XLA Modules:
  0.0 66.0 jit_solution(12354770347912367299)
XLA Ops:
  0.0 3.9 %pack_first.1 = (bf16[2,256,1024]{2,1,0:T(8,128)(2,1)}, bf16[4,3,64,512]{3,2,1,0:T(8,128)(2,1)S(1)}, bf16[4,3,64,512]{3,2,1,0:T(8,128)(2,1)S(1)}) custom-call(s32[2,4]{1,0:T(2,128)} %offsets.13, bf16[512,2048]{1,0:T(8,128)(2,1)} %q.3, bf16[512,2048]{1,0:T(8,128)(2,1)} %k.3, bf16[512,2048]{1,0:T(8,128)(2,1)} %v.3), custom_call_target="tpu_custom_call" | custom-call | flops 1000 | bytes 1000 | tf_op jit(solution)/shard_map/pack_first/pallas_call | solution.py:537
  3.9 0.8 %collective-permute-start = (bf16[4,3,64,512]{3,2,1,0:T(8,128)(2,1)S(1)}, bf16[4,3,64,512]{3,2,1,0:T(8,128)(2,1)S(1)}, u32[]{:S(2)}, u32[]{:S(2)}) collective-permute-start(bf16[4,3,64,512]{3,2,1,0:T(8,128)(2,1)S(1)} %get-tuple-element.23), channel_id=1, source_target_pairs={{0,1},{1,0},{2,3},{3,2},{4,5},{5,4},{6,7},{7,6},{8,9},{9,8},{10,11... | collective-permute-start | bytes 2359304 | tf_op jit(solution)/shard_map/ppermute | solution.py:65
  4.7 0.1 collective-permute-start.2
  4.8 0.4 collective-permute-start.3
  5.2 1.6 %collective-permute-done.received = bf16[4,3,64,512]{3,2,1,0:T(8,128)(2,1)S(1)} collective-permute-done((bf16[4,3,64,512]{3,2,1,0:T(8,128)(2,1)S(1)}, bf16[4,3,64,512]{3,2,1,0:T(8,128)(2,1)S(1)}, u32[]{:S(2)}, u32[]{:S(2)}) %collective-permute-start) | collective-permute-done | bytes 786464 | tf_op jit(solution)/shard_map/ppermute | solution.py:65
  6.8 0.4 collective-permute-start.1
  7.2 1.2 %collective-permute-start.5 = (bf16[2,256,1024]{2,1,0:T(8,128)(2,1)}, bf16[2,256,1024]{2,1,0:T(8,128)(2,1)S(1)}, u32[]{:S(2)}, u32[]{:S(2)}) collective-permute-start(bf16[2,256,1024]{2,1,0:T(8,128)(2,1)} %get-tuple-element.29), channel_id=1, source_target_pairs={{0,2},{1,3},{2,0},{3,1},{4,6},{5,7},{6,4},{7,5},{8,10},{9,11},{10,... | collective-permute-start | bytes 3145736 | tf_op jit(solution)/shard_map/ppermute | solution.py:65
  8.3 1.8 %pack_second.1 = bf16[16,3,64,128]{3,2,1,0:T(8,128)(2,1)} custom-call(s32[2,4]{1,0:T(2,128)} %offsets.13, bf16[4,3,64,512]{3,2,1,0:T(8,128)(2,1)S(1)} %get-tuple-element.22.kept, bf16[4,3,64,512]{3,2,1,0:T(8,128)(2,1)S(1)} %collective-permute-done.received), custom_call_target="tpu_custom_call" | custom-call | flops 1000 | bytes 1000 | tf_op jit(solution)/shard_map/pack_second/pallas_call | solution.py:537
  10.2 6.8 %all-to-all-start = ((bf16[16,3,64,128]{3,2,1,0:T(8,128)(2,1)}), bf16[16,3,64,128]{3,2,1,0:T(8,128)(2,1)}, u32[]{:S(2)}, u32[]{:S(2)}) async-start(bf16[16,3,64,128]{3,2,1,0:T(8,128)(2,1)} %pack_second.1), calls=%async_computation | async-start | bytes 1572864 | tf_op jit(solution)/shard_map/all_to_all | solution.py:564
  17.0 11.7 %local_kernel.1 = (bf16[256,2176]{1,0:T(8,128)(2,1)S(1)}, bf16[256,2176]{1,0:T(8,128)(2,1)}) custom-call(s32[2,4]{1,0:T(2,128)} %offsets.13, bf16[512,2048]{1,0:T(8,128)(2,1)} %q.3, bf16[512,2048]{1,0:T(8,128)(2,1)} %collective-permute-done.1.qo_in, bf16[512,2048]{1,0:T(8,128)(2,1)} %k.3, bf16[512,2048]{1,0:T(8,128)(2,1)} %collective-permute-done.2.ko_in.ko, ...), custom_call_target="tpu_custom_call" | custom-call | flops 10000000000 | bytes 1000 | tf_op jit(solution)/shard_map/local_kernel/pallas_call | solution.py:537
  28.7 1.1 %all-to-all-done.mine = bf16[16,3,64,128]{3,2,1,0:T(8,128)(2,1)} async-done(((bf16[16,3,64,128]{3,2,1,0:T(8,128)(2,1)}), bf16[16,3,64,128]{3,2,1,0:T(8,128)(2,1)}, u32[]{:S(2)}, u32[]{:S(2)}) %all-to-all-start) | async-done | bytes 786464 | tf_op jit(solution)/shard_map/all_to_all | solution.py:564
  29.8 2.7 %collective-permute-start.6 = (bf16[16,3,64,128]{3,2,1,0:T(8,128)(2,1)}, bf16[16,3,64,128]{3,2,1,0:T(8,128)(2,1)S(1)}, u32[]{:S(2)}, u32[]{:S(2)}) collective-permute-start(bf16[16,3,64,128]{3,2,1,0:T(8,128)(2,1)} %all-to-all-done.mine), channel_id=1, source_target_pairs={{0,1},{1,0},{2,3},{3,2},{4,5},{5,4},{6,7},{7,6},{8,9},{9,8},{10,11... | collective-permute-start | bytes 2359304 | tf_op jit(solution)/shard_map/ppermute | solution.py:65
  32.5 0.0 collective-permute-start.4
  32.5 2.1 %collective-permute-done.6.other = bf16[16,3,64,128]{3,2,1,0:T(8,128)(2,1)S(1)} collective-permute-done((bf16[16,3,64,128]{3,2,1,0:T(8,128)(2,1)}, bf16[16,3,64,128]{3,2,1,0:T(8,128)(2,1)S(1)}, u32[]{:S(2)}, u32[]{:S(2)}) %collective-permute-start.6) | collective-permute-done | bytes 786464 | tf_op jit(solution)/shard_map/ppermute | solution.py:65
  34.6 1.9 %far_kernel.1 = bf16[16,80,128]{2,1,0:T(8,128)(2,1)} custom-call(s32[2,4]{1,0:T(2,128)} %offsets.13, bf16[16,3,64,128]{3,2,1,0:T(8,128)(2,1)} %all-to-all-done.mine, bf16[16,3,64,128]{3,2,1,0:T(8,128)(2,1)S(1)} %collective-permute-done.6.other), custom_call_target="tpu_custom_call" | custom-call | flops 1000 | bytes 1000 | tf_op jit(solution)/shard_map/far_kernel/pallas_call | solution.py:537
  36.5 0.4 collective-permute-start.8
  36.9 5.0 %near_even.1 = bf16[256,1152]{1,0:T(8,128)(2,1)} custom-call(s32[2,4]{1,0:T(2,128)} %offsets.13, bf16[2,256,1024]{2,1,0:T(8,128)(2,1)S(1)} %collective-permute-done.5.qr.kv_a, bf16[512,2048]{1,0:T(8,128)(2,1)} %k.3, bf16[512,2048]{1,0:T(8,128)(2,1)} %collective-permute-done.2.ko_in.ko, bf16[512,2048]{1,0:T(8,128)(2,1)} %v.3, ...), custom_call_target="tpu_custom_call" | custom-call | flops 1000 | bytes 1000 | tf_op jit(solution)/shard_map/near_even/pallas_call | solution.py:537
  41.9 2.5 %collective-permute-start.7 = (bf16[256,1152]{1,0:T(8,128)(2,1)}, bf16[256,1152]{1,0:T(8,128)(2,1)}, u32[]{:S(2)}, u32[]{:S(2)}) collective-permute-start(bf16[256,1152]{1,0:T(8,128)(2,1)} %near_even.1), channel_id=1, source_target_pairs={{0,2},{1,3},{4,6},{5,7},{8,10},{9,11},{12,14},{13,15},{16,18},{17,... | collective-permute-start | bytes 1769480 | tf_op jit(solution)/shard_map/ppermute | solution.py:65
  44.3 7.1 %all-to-all-start.1 = ((bf16[16,80,128]{2,1,0:T(8,128)(2,1)}), bf16[16,80,128]{2,1,0:T(8,128)(2,1)}, u32[]{:S(2)}, u32[]{:S(2)}) async-start(bf16[16,80,128]{2,1,0:T(8,128)(2,1)} %far_kernel.1), calls=%async_computation.1 | async-start | bytes 655360 | tf_op jit(solution)/shard_map/all_to_all | solution.py:593
  51.4 3.6 %settle.1 = (bf16[512,2048]{1,0:T(8,128)(2,1)}, bf16[256,1152]{1,0:T(8,128)(2,1)}) custom-call(s32[2,4]{1,0:T(2,128)} %offsets.13, bf16[512,2048]{1,0:T(8,128)(2,1)} %q.3, bf16[2,256,1024]{2,1,0:T(8,128)(2,1)S(1)} %collective-permute-done.5.qr.kv_a, bf16[2,256,1024]{2,1,0:T(8,128)(2,1)} %collective-permute-done.8.kv_b, ...), custom_call_target="tpu_custom_call" | custom-call | flops 1000 | bytes 1000 | tf_op jit(solution)/shard_map/settle/pallas_call | solution.py:537
  55.0 4.6 %all-to-all-done.1.far_own = bf16[16,80,128]{2,1,0:T(8,128)(2,1)} async-done(((bf16[16,80,128]{2,1,0:T(8,128)(2,1)}), bf16[16,80,128]{2,1,0:T(8,128)(2,1)}, u32[]{:S(2)}, u32[]{:S(2)}) %all-to-all-start.1) | async-done | bytes 327712 | tf_op jit(solution)/shard_map/all_to_all | solution.py:593
  59.6 1.9 %collective-permute-start.9 = (bf16[16,80,128]{2,1,0:T(8,128)(2,1)}, bf16[16,80,128]{2,1,0:T(8,128)(2,1)S(1)}, u32[]{:S(2)}, u32[]{:S(2)}) collective-permute-start(bf16[16,80,128]{2,1,0:T(8,128)(2,1)} %all-to-all-done.1.far_own), channel_id=1, source_target_pairs={{0,1},{1,0},{2,3},{3,2},{4,5},{5,4},{6,7},{7,6},{8,9},{9,8},{10,11... | collective-permute-start | bytes 983048 | tf_op jit(solution)/shard_map/ppermute | solution.py:65
  61.6 1.5 %collective-permute-done.9.far_oth = bf16[16,80,128]{2,1,0:T(8,128)(2,1)S(1)} collective-permute-done((bf16[16,80,128]{2,1,0:T(8,128)(2,1)}, bf16[16,80,128]{2,1,0:T(8,128)(2,1)S(1)}, u32[]{:S(2)}, u32[]{:S(2)}) %collective-permute-start.9) | collective-permute-done | bytes 327712 | tf_op jit(solution)/shard_map/ppermute | solution.py:65
  63.0 2.8 %finish_kernel.1 = bf16[512,2048]{1,0:T(8,128)(2,1)} custom-call(s32[2,4]{1,0:T(2,128)} %offsets.13, bf16[256,2176]{1,0:T(8,128)(2,1)S(1)} %get-tuple-element.27.mine, bf16[256,2176]{1,0:T(8,128)(2,1)S(1)} %collective-permute-done.4.back, bf16[256,1152]{1,0:T(8,128)(2,1)} %collective-permute-done.7.near_a, ...), custom_call_target="tpu_custom_call", output_to_operand_aliasing={{}: (7, {})} | custom-call | flops 1000 | bytes 1000 | tf_op jit(solution)/shard_map/finish_kernel/pallas_call | solution.py:537
  (9 shorter events, 0.0 us)
Async XLA Ops:
  0.0 6.8 %copy-start = (bf16[512,2048]{1,0:T(8,128)(2,1)S(1)}, bf16[512,2048]{1,0:T(8,128)(2,1)}, u32[]{:S(2)}) copy-start(bf16[512,2048]{1,0:T(8,128)(2,1)} %q.3) | copy-start | bytes 6291460
  3.9 2.9 %collective-permute-start = (bf16[4,3,64,512]{3,2,1,0:T(8,128)(2,1)S(1)}, bf16[4,3,64,512]{3,2,1,0:T(8,128)(2,1)S(1)}, u32[]{:S(2)}, u32[]{:S(2)}) collective-permute-start(bf16[4,3,64,512]{3,2,1,0:T(8,128)(2,1)S(1)} %get-tuple-element.23), channel_id=1, source_target_pairs={{0,1},{1,0},{2,3},{3,2},{4,5},{5,4},{6,7},{7,6},{8,9},{9,8},{10,11... | collective-permute-start | bytes 2359304 | tf_op jit(solution)/shard_map/ppermute | solution.py:65
  4.7 12.3 %collective-permute-start.2 = (bf16[512,2048]{1,0:T(8,128)(2,1)}, bf16[512,2048]{1,0:T(8,128)(2,1)}, u32[]{:S(2)}, u32[]{:S(2)}) collective-permute-start(bf16[512,2048]{1,0:T(8,128)(2,1)} %k.3), channel_id=1, source_target_pairs={{0,1},{1,0},{2,3},{3,2},{4,5},{5,4},{6,7},{7,6},{8,9},{9,8},{10,11... | collective-permute-start | bytes 6291464 | tf_op jit(solution)/shard_map/ppermute | solution.py:65
  4.8 12.2 %collective-permute-start.3 = (bf16[512,2048]{1,0:T(8,128)(2,1)}, bf16[512,2048]{1,0:T(8,128)(2,1)}, u32[]{:S(2)}, u32[]{:S(2)}) collective-permute-start(bf16[512,2048]{1,0:T(8,128)(2,1)} %v.3), channel_id=1, source_target_pairs={{0,1},{1,0},{2,3},{3,2},{4,5},{5,4},{6,7},{7,6},{8,9},{9,8},{10,11... | collective-permute-start | bytes 6291464 | tf_op jit(solution)/shard_map/ppermute | solution.py:65
  6.8 10.2 %collective-permute-start.1 = (bf16[512,2048]{1,0:T(8,128)(2,1)S(1)}, bf16[512,2048]{1,0:T(8,128)(2,1)}, u32[]{:S(2)}, u32[]{:S(2)}) collective-permute-start(bf16[512,2048]{1,0:T(8,128)(2,1)S(1)} %copy-done), channel_id=1, source_target_pairs={{0,1},{1,0},{2,3},{3,2},{4,5},{5,4},{6,7},{7,6},{8,9},{9,8},{10,11... | collective-permute-start | bytes 6291464 | tf_op jit(solution)/shard_map/ppermute | solution.py:65
  7.2 29.4 %collective-permute-start.5 = (bf16[2,256,1024]{2,1,0:T(8,128)(2,1)}, bf16[2,256,1024]{2,1,0:T(8,128)(2,1)S(1)}, u32[]{:S(2)}, u32[]{:S(2)}) collective-permute-start(bf16[2,256,1024]{2,1,0:T(8,128)(2,1)} %get-tuple-element.29), channel_id=1, source_target_pairs={{0,2},{1,3},{2,0},{3,1},{4,6},{5,7},{6,4},{7,5},{8,10},{9,11},{10,... | collective-permute-start | bytes 3145736 | tf_op jit(solution)/shard_map/ppermute | solution.py:65
  10.2 19.6 %all-to-all-start = ((bf16[16,3,64,128]{3,2,1,0:T(8,128)(2,1)}), bf16[16,3,64,128]{3,2,1,0:T(8,128)(2,1)}, u32[]{:S(2)}, u32[]{:S(2)}) async-start(bf16[16,3,64,128]{3,2,1,0:T(8,128)(2,1)} %pack_second.1), calls=%async_computation | async-start | bytes 1572864 | tf_op jit(solution)/shard_map/all_to_all | solution.py:564
  29.8 4.9 %collective-permute-start.6 = (bf16[16,3,64,128]{3,2,1,0:T(8,128)(2,1)}, bf16[16,3,64,128]{3,2,1,0:T(8,128)(2,1)S(1)}, u32[]{:S(2)}, u32[]{:S(2)}) collective-permute-start(bf16[16,3,64,128]{3,2,1,0:T(8,128)(2,1)} %all-to-all-done.mine), channel_id=1, source_target_pairs={{0,1},{1,0},{2,3},{3,2},{4,5},{5,4},{6,7},{7,6},{8,9},{9,8},{10,11... | collective-permute-start | bytes 2359304 | tf_op jit(solution)/shard_map/ppermute | solution.py:65
  32.5 18.9 %collective-permute-start.4 = (bf16[256,2176]{1,0:T(8,128)(2,1)}, bf16[256,2176]{1,0:T(8,128)(2,1)S(1)}, u32[]{:S(2)}, u32[]{:S(2)}) collective-permute-start(bf16[256,2176]{1,0:T(8,128)(2,1)} %get-tuple-element.28), channel_id=1, source_target_pairs={{0,1},{1,0},{2,3},{3,2},{4,5},{5,4},{6,7},{7,6},{8,9},{9,8},{10,11... | collective-permute-start | bytes 3342344 | tf_op jit(solution)/shard_map/ppermute | solution.py:65
  36.5 14.9 %collective-permute-start.8 = (bf16[2,256,1024]{2,1,0:T(8,128)(2,1)S(1)}, bf16[2,256,1024]{2,1,0:T(8,128)(2,1)}, u32[]{:S(2)}, u32[]{:S(2)}) collective-permute-start(bf16[2,256,1024]{2,1,0:T(8,128)(2,1)S(1)} %collective-permute-done.5.qr.kv_a), channel_id=1, source_target_pairs={{0,1},{1,0},{2,3},{3,2},{4,5},{5,4},{6,7},{7,6},{8,9},{9,8},{10,11... | collective-permute-start | bytes 3145736 | tf_op jit(solution)/shard_map/ppermute | solution.py:65
  41.9 17.8 %collective-permute-start.7 = (bf16[256,1152]{1,0:T(8,128)(2,1)}, bf16[256,1152]{1,0:T(8,128)(2,1)}, u32[]{:S(2)}, u32[]{:S(2)}) collective-permute-start(bf16[256,1152]{1,0:T(8,128)(2,1)} %near_even.1), channel_id=1, source_target_pairs={{0,2},{1,3},{4,6},{5,7},{8,10},{9,11},{12,14},{13,15},{16,18},{17,... | collective-permute-start | bytes 1769480 | tf_op jit(solution)/shard_map/ppermute | solution.py:65
  44.3 15.3 %all-to-all-start.1 = ((bf16[16,80,128]{2,1,0:T(8,128)(2,1)}), bf16[16,80,128]{2,1,0:T(8,128)(2,1)}, u32[]{:S(2)}, u32[]{:S(2)}) async-start(bf16[16,80,128]{2,1,0:T(8,128)(2,1)} %far_kernel.1), calls=%async_computation.1 | async-start | bytes 655360 | tf_op jit(solution)/shard_map/all_to_all | solution.py:593
  59.6 3.4 %collective-permute-start.9 = (bf16[16,80,128]{2,1,0:T(8,128)(2,1)}, bf16[16,80,128]{2,1,0:T(8,128)(2,1)S(1)}, u32[]{:S(2)}, u32[]{:S(2)}) collective-permute-start(bf16[16,80,128]{2,1,0:T(8,128)(2,1)} %all-to-all-done.1.far_own), channel_id=1, source_target_pairs={{0,1},{1,0},{2,3},{3,2},{4,5},{5,4},{6,7},{7,6},{8,9},{9,8},{10,11... | collective-permute-start | bytes 983048 | tf_op jit(solution)/shard_map/ppermute | solution.py:65
where the time goes:
time: 67 us; the launch traced here: 66 us
  Pallas kernels  30.6 us (46%)
  starting transfers between devices  24.2 us (36%)
  waiting for transfers between devices  10.9 us (16%)
    pallas_call x7, Pallas kernels, call(): pl.pallas_call(kernel, out_shape=outs, in_specs=[SMEM] + places, out_spec...  30.6 us
    ppermute x10, starting transfers between devices, move(): return lax.ppermute(array, AXES, pairs)  10.3 us
    all_to_all x1, starting transfers between devices, device_part(): far_back = lax.all_to_all(far_out, ('x', 'y'), 0, 0, tiled=True)  7.07 us
    all_to_all x1, starting transfers between devices, device_part(): far_mine = lax.all_to_all(far_pack, ('x', 'y'), 0, 0, tiled=True)  6.8 us
    ppermute x10, waiting for transfers between devices, move(): return lax.ppermute(array, AXES, pairs)  5.19 us
    all_to_all x1, waiting for transfers between devices, device_part(): far_back = lax.all_to_all(far_out, ('x', 'y'), 0, 0, tiled=True)  4.63 us
  transfers between devices with their start and end apart: 12, of which 5 were waited for; matrix products, arithmetic and copies ran while one was open for 0% of the time, Pallas kernels for 36%

commit v1 on v0

--- a/solution.py
+++ b/solution.py
@@ -18,6 +18,7 @@
 GW = GH * HD
 ROWS = 512
 NSEL = 256
+ASK = 3
 AXES = ("x", "y", "z", "c")
 SIZES = (4, 4, 4, 2)
 SCALE = float(HD**-0.5 * np.log2(np.e))
@@ -125,18 +126,17 @@
         @pl.when(here.odd == odd)
         def _():
             nears = []
-            for g in range(2):
+            pieces = [(q, g, g) for g in range(ASK)] if odd else [(k, ASK, 0), (v, ASK, 1)]
+            for source, g, place in pieces:
                 for half in range(2):
-                    rows = rows_at((here.near(g if odd else g + 2) + 2 * half) * BLK, BLK)
-                    to = pl.ds(half * BLK, BLK)
-                    for t, source in enumerate((q,) if odd else (k, v)):
-                        nears.append(
-                            pltpu.make_async_copy(
-                                source.at[rows, group_cols(g if odd else g + 2)],
-                                near.at[t, to, group_cols(g)],
-                                sems.at[len(copies) + len(nears)],
-                            )
+                    rows = rows_at((here.near(g) + 2 * half) * BLK, BLK)
+                    nears.append(
+                        pltpu.make_async_copy(
+                            source.at[rows, group_cols(g)],
+                            near.at[pl.ds(half * BLK, BLK), group_cols(place)],
+                            sems.at[len(copies) + len(nears)],
                         )
+                    )
             run_copies(copies + nears)
 
 
@@ -191,7 +191,7 @@
     @pl.when(jnp.logical_not(here.odd))
     def _():
         copies = []
-        for g in range(2):
+        for g in range(ASK):
             for n, (source, half) in enumerate([(0, 0), (0, 1), (1, 0), (1, 1)]):
                 rows = rows_at((here.near(g) + 2 * half) * BLK, BLK)
                 for two, target in (((k, ko), keys), ((v, vo), vals)):
@@ -204,8 +204,8 @@
                     )
         run_copies(copies)
         near_part(
-            2 * GH,
-            lambda h: qr[0, :, head_cols(h)],
+            ASK * GH,
+            lambda h: qr[:, head_cols(h)],
             lambda h: [keys[:, head_cols(h)]],
             lambda h: [vals[:, head_cols(h)]],
             out,
@@ -390,10 +390,10 @@
 
 def next_part(nears, half, g, h):
     rows = slice(half * BLK, (half + 1) * BLK)
-    source, place = nears[g // 2], (g % 2) * GH + h
+    source, place, heads = (nears[0], g * GH + h, ASK * GH) if g < ASK else (nears[1], h, GH)
     return (
         source[rows, head_cols(place)].astype(F32),
-        spread_lanes(source[rows, 2 * GW :], [n * 2 * GH + place for n in range(3)]),
+        spread_lanes(source[rows, heads * HD :], [n * heads + place for n in range(3)]),
     )
 
 
@@ -401,16 +401,13 @@
     here = Place(offsets)
     halves = (mine, back)
     copies = []
-    for g in range(2):
-        for half in range(2):
-            rows = rows_at((here.near(2 + g) + 2 * half) * BLK, BLK)
-            copies.append(
-                pltpu.make_async_copy(
-                    q.at[rows, group_cols(2 + g)],
-                    queries.at[pl.ds(half * BLK, BLK), group_cols(g)],
-                    sems.at[len(copies)],
-                )
+    for half in range(2):
+        rows = rows_at((here.near(ASK) + 2 * half) * BLK, BLK)
+        copies.append(
+            pltpu.make_async_copy(
+                q.at[rows, group_cols(ASK)], queries.at[pl.ds(half * BLK, BLK)], sems.at[len(copies)]
             )
+        )
 
     @pl.when(here.odd)
     def _():
@@ -423,30 +420,28 @@
     def leave(g):
         return pltpu.make_async_copy(done.at[:, group_cols(g)], out.at[:, group_cols(g)], out_sems.at[g])
 
-    leave(0).start()
-    leave(1).start()
+    for g in range(ASK):
+        leave(g).start()
 
     @pl.when(here.odd)
     def _():
         for c in copies:
             c.wait()
         near_part(
-            2 * GH,
+            GH,
             lambda h: queries[:, head_cols(h)],
-            lambda h: [r[0, :, head_cols(h)] for r in (kv_a, kv_b)],
-            lambda h: [r[1, :, head_cols(h)] for r in (kv_a, kv_b)],
+            lambda h: [r[:, head_cols(h)] for r in (kv_a, kv_b)],
+            lambda h: [r[:, head_cols(GH + h)] for r in (kv_a, kv_b)],
             near,
         )
-        for g in (2, 3):
-            rows = rows_at(here.near(g) * BLK, BLK)
-            for half in range(2):
-                to = rows_at(here.near(g) * BLK + half * NSEL, BLK)
-                for h in range(GH):
-                    parts = [own_part(halves, half, rows, g, h), next_part((None, near), half, g, h)]
-                    done[to, pl.ds(g * GW + h * HD, HD)] = mix(parts)
-
-    leave(2).start()
-    leave(3).start()
+        rows = rows_at(here.near(ASK) * BLK, BLK)
+        for half in range(2):
+            to = rows_at(here.near(ASK) * BLK + half * NSEL, BLK)
+            for h in range(GH):
+                parts = [own_part(halves, half, rows, ASK, h), next_part((None, near), half, ASK, h)]
+                done[to, pl.ds(ASK * GW + h * HD, HD)] = mix(parts)
+
+    leave(ASK).start()
     for g in range(GROUPS):
         leave(g).wait()
 
@@ -456,7 +451,7 @@
 ):
     here = Place(offsets)
     nears, halves = (near_a, near_b), (mine, back)
-    want_near_b = here.odd & (here.far_here(2) | here.far_here(3))
+    want_near_b = here.odd & here.far_here(ASK)
     fetch = pltpu.make_async_copy(near_in, near_b, sem)
 
     @pl.when(want_near_b)
@@ -474,7 +469,7 @@
     def near_here(g, half):
         return here.odd & jnp.logical_not(here.far_here(g) & (here.far_block(g) == here.near(g) + 2 * half))
 
-    for g in range(2):
+    for g in range(ASK):
         rows = rows_at(here.near(g) * BLK, BLK)
         for half in range(2):
 
@@ -510,7 +505,7 @@
         def _():
             far_copy(g).wait()
 
-    for g in range(2):
+    for g in range(ASK):
         for half in range(2):
 
             @pl.when(near_here(g, half))
@@ -550,10 +545,10 @@
     half_shape = shape(GROUPS, 3, HALF, GW)
     near_x, far_send, far_keep = call(
         pack_first,
-        [pltpu.VMEM((2, NSEL, 2 * GW), BF), half_shape, half_shape],
+        [shape(NSEL, ASK * GW), half_shape, half_shape],
         (qh, kh, vh),
         [HBM] * 3,
-        sems=6 * GROUPS + 8,
+        sems=6 * GROUPS + 2 * ASK,
         out_places=[VMEM] * 3,
     )
     far_recv = move(far_send, CORE)
@@ -575,31 +570,29 @@
         flops=10**10,
     )
     back = move(away, CORE)
-    far_mine, mine = lax.optimization_barrier((far_mine, mine))
-    far_other = move(far_mine, CORE)
-    far_out = call(far_kernel, pltpu.HBM((HEADS, HALF + 16, HD), BF), (far_mine, far_other), [VMEM] * 2)
-    near_r, far_out = lax.optimization_barrier((near_r, far_out))
-    near_ro = move(near_r, CORE)
+    near_r, far_mine, mine = lax.optimization_barrier((near_r, far_mine, mine))
+    far_other, near_ro = move(far_mine, CORE), move(near_r, CORE)
     near_out = call(
         near_even,
-        shape(NSEL, 2 * GW + HD),
+        shape(NSEL, ASK * GW + HD),
         (near_r, kh, ko, vh, vo),
         [VMEM] + [HBM] * 4,
-        sems=16,
-        scratch=[pltpu.VMEM((ROWS, 2 * GW), BF)] * 2,
+        sems=8 * ASK,
+        scratch=[pltpu.VMEM((ROWS, ASK * GW), BF)] * 2,
     )
     near_back = move(near_out, TO_ODD)
-    far_out, near_out = lax.optimization_barrier((far_out, near_out))
+    far_other, near_out = lax.optimization_barrier((far_other, near_out))
+    far_out = call(far_kernel, pltpu.HBM((HEADS, HALF + 16, HD), BF), (far_mine, far_other), [VMEM] * 2)
     far_back = lax.all_to_all(far_out, ("x", "y"), 0, 0, tiled=True)
     out, near_here = call(
         settle,
-        [shape(ROWS, HEADS * HD), pltpu.HBM((NSEL, 2 * GW + HD), BF)],
+        [shape(ROWS, HEADS * HD), pltpu.HBM((NSEL, GW + HD), BF)],
         (qh, near_r, near_ro, mine, back),
         [HBM] + [VMEM] * 4,
         scratch=[
-            pltpu.VMEM((NSEL, 2 * GW), BF),
+            pltpu.VMEM((NSEL, GW), BF),
             pltpu.VMEM((ROWS, HEADS * HD), BF),
-            pltpu.SemaphoreType.DMA((4,)),
+            pltpu.SemaphoreType.DMA((2,)),
             pltpu.SemaphoreType.DMA((GROUPS,)),
         ],
         out_places=[HBM, VMEM],
@@ -613,10 +606,10 @@
         (mine, back, near_back, far_back, far_back_other, near_here, out),
         [VMEM] * 5 + [HBM] * 2,
         scratch=[
-            pltpu.VMEM((2, 2, BLK, GW), BF),
+            pltpu.VMEM((ASK, 2, BLK, GW), BF),
             pltpu.VMEM((GROUPS, BLK, GW), BF),
-            pltpu.VMEM((NSEL, 2 * GW + HD), BF),
-            pltpu.SemaphoreType.DMA((2, 2)),
+            pltpu.VMEM((NSEL, GW + HD), BF),
+            pltpu.SemaphoreType.DMA((ASK, 2)),
             pltpu.SemaphoreType.DMA((GROUPS,)),
             pltpu.SemaphoreType.DMA,
         ],

time: 67 us -> 66.9 us (level)
  the two profiles are of different devices: /device:TPU:65 before, /device:TPU:97 now
where the time goes in v1:
time: 66.9 us; the launch traced here: 66.2 us
  Pallas kernels  31.2 us (47%)
  starting transfers between devices  22 us (33%)
  waiting for transfers between devices  12.8 us (19%)
    pallas_call x7, Pallas kernels, call(): pl.pallas_call(kernel, out_shape=outs, in_specs=[SMEM] + places, out_spec...  31.2 us
    ppermute x10, waiting for transfers between devices, move(): return lax.ppermute(array, AXES, pairs)  12.7 us
    all_to_all x1, starting transfers between devices, device_part(): far_back = lax.all_to_all(far_out, ('x', 'y'), 0, 0, tiled=True)  7.96 us
    ppermute x10, starting transfers between devices, move(): return lax.ppermute(array, AXES, pairs)  7.32 us
    all_to_all x1, starting transfers between devices, device_part(): far_mine = lax.all_to_all(far_pack, ('x', 'y'), 0, 0, tiled=True)  6.75 us
  transfers between devices with their start and end apart: 12, of which 4 were waited for; matrix products, arithmetic and copies ran while one was open for 0% of the time, Pallas kernels for 35%

profile of v1, /device:TPU:97, one launch (start us, length us, event | category | flops | bytes accessed | tf_op | source)
XLA Modules:
  0.0 66.2 jit_solution(616432438871870426)
XLA Ops:
  0.0 3.7 %pack_first.1 = (bf16[256,1536]{1,0:T(8,128)(2,1)}, bf16[4,3,64,512]{3,2,1,0:T(8,128)(2,1)S(1)}, bf16[4,3,64,512]{3,2,1,0:T(8,128)(2,1)S(1)}) custom-call(s32[2,4]{1,0:T(2,128)} %offsets.13, bf16[512,2048]{1,0:T(8,128)(2,1)} %q.3, bf16[512,2048]{1,0:T(8,128)(2,1)} %k.3, bf16[512,2048]{1,0:T(8,128)(2,1)} %v.3), custom_call_target="tpu_custom_call" | custom-call | flops 1000 | bytes 1000 | tf_op jit(solution)/shard_map/pack_first/pallas_call | solution.py:532
  3.7 0.8 %collective-permute-start.1 = (bf16[4,3,64,512]{3,2,1,0:T(8,128)(2,1)S(1)}, bf16[4,3,64,512]{3,2,1,0:T(8,128)(2,1)S(1)}, u32[]{:S(2)}, u32[]{:S(2)}) collective-permute-start(bf16[4,3,64,512]{3,2,1,0:T(8,128)(2,1)S(1)} %get-tuple-element.23), channel_id=1, source_target_pairs={{0,1},{1,0},{2,3},{3,2},{4,5},{5,4},{6,7},{7,6},{8,9},{9,8},{10,11... | collective-permute-start | bytes 2359304 | tf_op jit(solution)/shard_map/ppermute | solution.py:66
  4.5 0.1 collective-permute-start.3
  4.5 0.4 collective-permute-start.4
  5.0 1.6 %collective-permute-done.1.received = bf16[4,3,64,512]{3,2,1,0:T(8,128)(2,1)S(1)} collective-permute-done((bf16[4,3,64,512]{3,2,1,0:T(8,128)(2,1)S(1)}, bf16[4,3,64,512]{3,2,1,0:T(8,128)(2,1)S(1)}, u32[]{:S(2)}, u32[]{:S(2)}) %collective-permute-start.1) | collective-permute-done | bytes 786464 | tf_op jit(solution)/shard_map/ppermute | solution.py:66
  6.6 0.4 collective-permute-start.2
  6.9 0.0 collective-permute-start
  7.0 1.9 %pack_second.1 = bf16[16,3,64,128]{3,2,1,0:T(8,128)(2,1)} custom-call(s32[2,4]{1,0:T(2,128)} %offsets.13, bf16[4,3,64,512]{3,2,1,0:T(8,128)(2,1)S(1)} %get-tuple-element.22.kept, bf16[4,3,64,512]{3,2,1,0:T(8,128)(2,1)S(1)} %collective-permute-done.1.received), custom_call_target="tpu_custom_call" | custom-call | flops 1000 | bytes 1000 | tf_op jit(solution)/shard_map/pack_second/pallas_call | solution.py:532
  8.8 6.8 %all-to-all-start = ((bf16[16,3,64,128]{3,2,1,0:T(8,128)(2,1)}), bf16[16,3,64,128]{3,2,1,0:T(8,128)(2,1)S(1)}, u32[]{:S(2)}, u32[]{:S(2)}) async-start(bf16[16,3,64,128]{3,2,1,0:T(8,128)(2,1)} %pack_second.1), calls=%async_computation | async-start | bytes 1572864 | tf_op jit(solution)/shard_map/all_to_all | solution.py:559
  15.6 0.0 collective-permute-done.3.ko_in.ko
  15.6 0.1 collective-permute-done.4.vo_in.vo
  15.7 11.7 %local_kernel.1 = (bf16[256,2176]{1,0:T(8,128)(2,1)S(1)}, bf16[256,2176]{1,0:T(8,128)(2,1)}) custom-call(s32[2,4]{1,0:T(2,128)} %offsets.13, bf16[512,2048]{1,0:T(8,128)(2,1)} %q.3, bf16[512,2048]{1,0:T(8,128)(2,1)} %collective-permute-done.2.qo_in, bf16[512,2048]{1,0:T(8,128)(2,1)} %k.3, bf16[512,2048]{1,0:T(8,128)(2,1)} %collective-permute-done.3.ko_in.ko, ...), custom_call_target="tpu_custom_call" | custom-call | flops 10000000000 | bytes 1000 | tf_op jit(solution)/shard_map/local_kernel/pallas_call | solution.py:532
  27.4 1.8 %collective-permute-start.5 = (bf16[256,2176]{1,0:T(8,128)(2,1)}, bf16[256,2176]{1,0:T(8,128)(2,1)S(1)}, u32[]{:S(2)}, u32[]{:S(2)}) collective-permute-start(bf16[256,2176]{1,0:T(8,128)(2,1)} %get-tuple-element.28), channel_id=1, source_target_pairs={{0,1},{1,0},{2,3},{3,2},{4,5},{5,4},{6,7},{7,6},{8,9},{9,8},{10,11... | collective-permute-start | bytes 3342344 | tf_op jit(solution)/shard_map/ppermute | solution.py:66
  29.2 1.9 %collective-permute-start.6 = (bf16[16,3,64,128]{3,2,1,0:T(8,128)(2,1)S(1)}, bf16[16,3,64,128]{3,2,1,0:T(8,128)(2,1)S(1)}, u32[]{:S(2)}, u32[]{:S(2)}) collective-permute-start(bf16[16,3,64,128]{3,2,1,0:T(8,128)(2,1)S(1)} %all-to-all-done.mine), channel_id=1, source_target_pairs={{0,1},{1,0},{2,3},{3,2},{4,5},{5,4},{6,7},{7,6},{8,9},{9,8},{10,11... | collective-permute-start | bytes 2359304 | tf_op jit(solution)/shard_map/ppermute | solution.py:66
  31.1 2.3 %near_even.1 = bf16[256,1664]{1,0:T(8,128)(2,1)} custom-call(s32[2,4]{1,0:T(2,128)} %offsets.13, bf16[256,1536]{1,0:T(8,128)(2,1)} %collective-permute-done.qr.kv_a, bf16[512,2048]{1,0:T(8,128)(2,1)} %k.3, bf16[512,2048]{1,0:T(8,128)(2,1)} %collective-permute-done.3.ko_in.ko, bf16[512,2048]{1,0:T(8,128)(2,1)} %v.3, ...), custom_call_target="tpu_custom_call" | custom-call | flops 1000 | bytes 1000 | tf_op jit(solution)/shard_map/near_even/pallas_call | solution.py:532
  33.4 1.3 %collective-permute-start.7 = (bf16[256,1664]{1,0:T(8,128)(2,1)}, bf16[256,1664]{1,0:T(8,128)(2,1)}, u32[]{:S(2)}, u32[]{:S(2)}) collective-permute-start(bf16[256,1664]{1,0:T(8,128)(2,1)} %near_even.1), channel_id=1, source_target_pairs={{0,2},{1,3},{4,6},{5,7},{8,10},{9,11},{12,14},{13,15},{16,18},{17,... | collective-permute-start | bytes 2555912 | tf_op jit(solution)/shard_map/ppermute | solution.py:66
  34.7 0.1 collective-permute-start.8
  34.8 1.6 %far_kernel.1 = bf16[16,80,128]{2,1,0:T(8,128)(2,1)} custom-call(s32[2,4]{1,0:T(2,128)} %offsets.13, bf16[16,3,64,128]{3,2,1,0:T(8,128)(2,1)S(1)} %all-to-all-done.mine, bf16[16,3,64,128]{3,2,1,0:T(8,128)(2,1)S(1)} %collective-permute-done.6.other), custom_call_target="tpu_custom_call" | custom-call | flops 1000 | bytes 1000 | tf_op jit(solution)/shard_map/far_kernel/pallas_call | solution.py:532
  36.4 8.0 %all-to-all-start.1 = ((bf16[16,80,128]{2,1,0:T(8,128)(2,1)}), bf16[16,80,128]{2,1,0:T(8,128)(2,1)S(1)}, u32[]{:S(2)}, u32[]{:S(2)}) async-start(bf16[16,80,128]{2,1,0:T(8,128)(2,1)} %far_kernel.1), calls=%async_computation.1 | async-start | bytes 655360 | tf_op jit(solution)/shard_map/all_to_all | solution.py:586
  44.4 5.6 %settle.1 = (bf16[512,2048]{1,0:T(8,128)(2,1)}, bf16[256,640]{1,0:T(8,128)(2,1)}) custom-call(s32[2,4]{1,0:T(2,128)} %offsets.13, bf16[512,2048]{1,0:T(8,128)(2,1)} %q.3, bf16[256,1536]{1,0:T(8,128)(2,1)} %collective-permute-done.qr.kv_a, bf16[256,1536]{1,0:T(8,128)(2,1)} %collective-permute-done.8.kv_b, bf16[256,2176]{1,0:T(8,128)(2,1)S(1)} %get-tuple-element.27.mine, ...), custom_call_target="tpu_custom_call" | custom-call | flops 1000 | bytes 1000 | tf_op jit(solution)/shard_map/settle/pallas_call | solution.py:532
  50.0 9.8 %collective-permute-done.7.near_a = bf16[256,1664]{1,0:T(8,128)(2,1)} collective-permute-done((bf16[256,1664]{1,0:T(8,128)(2,1)}, bf16[256,1664]{1,0:T(8,128)(2,1)}, u32[]{:S(2)}, u32[]{:S(2)}) %collective-permute-start.7) | collective-permute-done | bytes 852000 | tf_op jit(solution)/shard_map/ppermute | solution.py:66
  59.8 0.6 collective-permute-start.9
  60.4 1.3 %collective-permute-done.9.far_oth = bf16[16,80,128]{2,1,0:T(8,128)(2,1)S(1)} collective-permute-done((bf16[16,80,128]{2,1,0:T(8,128)(2,1)S(1)}, bf16[16,80,128]{2,1,0:T(8,128)(2,1)S(1)}, u32[]{:S(2)}, u32[]{:S(2)}) %collective-permute-start.9) | collective-permute-done | bytes 327712 | tf_op jit(solution)/shard_map/ppermute | solution.py:66
  61.7 4.4 %finish_kernel.1 = bf16[512,2048]{1,0:T(8,128)(2,1)} custom-call(s32[2,4]{1,0:T(2,128)} %offsets.13, bf16[256,2176]{1,0:T(8,128)(2,1)S(1)} %get-tuple-element.27.mine, bf16[256,2176]{1,0:T(8,128)(2,1)S(1)} %collective-permute-done.5.back, bf16[256,1664]{1,0:T(8,128)(2,1)} %collective-permute-done.7.near_a, ...), custom_call_target="tpu_custom_call", output_to_operand_aliasing={{}: (7, {})} | custom-call | flops 1000 | bytes 1000 | tf_op jit(solution)/shard_map/finish_kernel/pallas_call | solution.py:532
  (9 shorter events, 0.0 us)
Async XLA Ops:
  0.0 6.6 %copy-start = (bf16[512,2048]{1,0:T(8,128)(2,1)S(1)}, bf16[512,2048]{1,0:T(8,128)(2,1)}, u32[]{:S(2)}) copy-start(bf16[512,2048]{1,0:T(8,128)(2,1)} %q.3) | copy-start | bytes 6291460
  3.7 2.9 %collective-permute-start.1 = (bf16[4,3,64,512]{3,2,1,0:T(8,128)(2,1)S(1)}, bf16[4,3,64,512]{3,2,1,0:T(8,128)(2,1)S(1)}, u32[]{:S(2)}, u32[]{:S(2)}) collective-permute-start(bf16[4,3,64,512]{3,2,1,0:T(8,128)(2,1)S(1)} %get-tuple-element.23), channel_id=1, source_target_pairs={{0,1},{1,0},{2,3},{3,2},{4,5},{5,4},{6,7},{7,6},{8,9},{9,8},{10,11... | collective-permute-start | bytes 2359304 | tf_op jit(solution)/shard_map/ppermute | solution.py:66
  4.5 11.1 %collective-permute-start.3 = (bf16[512,2048]{1,0:T(8,128)(2,1)}, bf16[512,2048]{1,0:T(8,128)(2,1)}, u32[]{:S(2)}, u32[]{:S(2)}) collective-permute-start(bf16[512,2048]{1,0:T(8,128)(2,1)} %k.3), channel_id=1, source_target_pairs={{0,1},{1,0},{2,3},{3,2},{4,5},{5,4},{6,7},{7,6},{8,9},{9,8},{10,11... | collective-permute-start | bytes 6291464 | tf_op jit(solution)/shard_map/ppermute | solution.py:66
  4.5 11.2 %collective-permute-start.4 = (bf16[512,2048]{1,0:T(8,128)(2,1)}, bf16[512,2048]{1,0:T(8,128)(2,1)}, u32[]{:S(2)}, u32[]{:S(2)}) collective-permute-start(bf16[512,2048]{1,0:T(8,128)(2,1)} %v.3), channel_id=1, source_target_pairs={{0,1},{1,0},{2,3},{3,2},{4,5},{5,4},{6,7},{7,6},{8,9},{9,8},{10,11... | collective-permute-start | bytes 6291464 | tf_op jit(solution)/shard_map/ppermute | solution.py:66
  6.6 9.1 %collective-permute-start.2 = (bf16[512,2048]{1,0:T(8,128)(2,1)S(1)}, bf16[512,2048]{1,0:T(8,128)(2,1)}, u32[]{:S(2)}, u32[]{:S(2)}) collective-permute-start(bf16[512,2048]{1,0:T(8,128)(2,1)S(1)} %copy-done), channel_id=1, source_target_pairs={{0,1},{1,0},{2,3},{3,2},{4,5},{5,4},{6,7},{7,6},{8,9},{9,8},{10,11... | collective-permute-start | bytes 6291464 | tf_op jit(solution)/shard_map/ppermute | solution.py:66
  6.9 22.2 %collective-permute-start = (bf16[256,1536]{1,0:T(8,128)(2,1)}, bf16[256,1536]{1,0:T(8,128)(2,1)}, u32[]{:S(2)}, u32[]{:S(2)}) collective-permute-start(bf16[256,1536]{1,0:T(8,128)(2,1)} %get-tuple-element.21), channel_id=1, source_target_pairs={{0,2},{1,3},{2,0},{3,1},{4,6},{5,7},{6,4},{7,5},{8,10},{9,11},{10,... | collective-permute-start | bytes 2359304 | tf_op jit(solution)/shard_map/ppermute | solution.py:66
  8.8 20.3 %all-to-all-start = ((bf16[16,3,64,128]{3,2,1,0:T(8,128)(2,1)}), bf16[16,3,64,128]{3,2,1,0:T(8,128)(2,1)S(1)}, u32[]{:S(2)}, u32[]{:S(2)}) async-start(bf16[16,3,64,128]{3,2,1,0:T(8,128)(2,1)} %pack_second.1), calls=%async_computation | async-start | bytes 1572864 | tf_op jit(solution)/shard_map/all_to_all | solution.py:559
  27.4 17.0 %collective-permute-start.5 = (bf16[256,2176]{1,0:T(8,128)(2,1)}, bf16[256,2176]{1,0:T(8,128)(2,1)S(1)}, u32[]{:S(2)}, u32[]{:S(2)}) collective-permute-start(bf16[256,2176]{1,0:T(8,128)(2,1)} %get-tuple-element.28), channel_id=1, source_target_pairs={{0,1},{1,0},{2,3},{3,2},{4,5},{5,4},{6,7},{7,6},{8,9},{9,8},{10,11... | collective-permute-start | bytes 3342344 | tf_op jit(solution)/shard_map/ppermute | solution.py:66
  29.2 5.6 %collective-permute-start.6 = (bf16[16,3,64,128]{3,2,1,0:T(8,128)(2,1)S(1)}, bf16[16,3,64,128]{3,2,1,0:T(8,128)(2,1)S(1)}, u32[]{:S(2)}, u32[]{:S(2)}) collective-permute-start(bf16[16,3,64,128]{3,2,1,0:T(8,128)(2,1)S(1)} %all-to-all-done.mine), channel_id=1, source_target_pairs={{0,1},{1,0},{2,3},{3,2},{4,5},{5,4},{6,7},{7,6},{8,9},{9,8},{10,11... | collective-permute-start | bytes 2359304 | tf_op jit(solution)/shard_map/ppermute | solution.py:66
  33.4 26.5 %collective-permute-start.7 = (bf16[256,1664]{1,0:T(8,128)(2,1)}, bf16[256,1664]{1,0:T(8,128)(2,1)}, u32[]{:S(2)}, u32[]{:S(2)}) collective-permute-start(bf16[256,1664]{1,0:T(8,128)(2,1)} %near_even.1), channel_id=1, source_target_pairs={{0,2},{1,3},{4,6},{5,7},{8,10},{9,11},{12,14},{13,15},{16,18},{17,... | collective-permute-start | bytes 2555912 | tf_op jit(solution)/shard_map/ppermute | solution.py:66
  34.7 9.7 %collective-permute-start.8 = (bf16[256,1536]{1,0:T(8,128)(2,1)}, bf16[256,1536]{1,0:T(8,128)(2,1)}, u32[]{:S(2)}, u32[]{:S(2)}) collective-permute-start(bf16[256,1536]{1,0:T(8,128)(2,1)} %collective-permute-done.qr.kv_a), channel_id=1, source_target_pairs={{0,1},{1,0},{2,3},{3,2},{4,5},{5,4},{6,7},{7,6},{8,9},{9,8},{10,11... | collective-permute-start | bytes 2359304 | tf_op jit(solution)/shard_map/ppermute | solution.py:66
  36.4 23.4 %all-to-all-start.1 = ((bf16[16,80,128]{2,1,0:T(8,128)(2,1)}), bf16[16,80,128]{2,1,0:T(8,128)(2,1)S(1)}, u32[]{:S(2)}, u32[]{:S(2)}) async-start(bf16[16,80,128]{2,1,0:T(8,128)(2,1)} %far_kernel.1), calls=%async_computation.1 | async-start | bytes 655360 | tf_op jit(solution)/shard_map/all_to_all | solution.py:586
  59.8 1.8 %collective-permute-start.9 = (bf16[16,80,128]{2,1,0:T(8,128)(2,1)S(1)}, bf16[16,80,128]{2,1,0:T(8,128)(2,1)S(1)}, u32[]{:S(2)}, u32[]{:S(2)}) collective-permute-start(bf16[16,80,128]{2,1,0:T(8,128)(2,1)S(1)} %all-to-all-done.1.far_own), channel_id=1, source_target_pairs={{0,1},{1,0},{2,3},{3,2},{4,5},{5,4},{6,7},{7,6},{8,9},{9,8},{10,11... | collective-permute-start | bytes 983048 | tf_op jit(solution)/shard_map/ppermute | solution.py:66

commit v2 on v1

--- a/solution.py
+++ b/solution.py
@@ -173,15 +173,27 @@
     return slice(h * HD, (h + 1) * HD)
 
 
-def near_part(heads, q_of, keys_of, vals_of, out):
+def near_part(heads, q_of, keys_of, vals_of, out, ready=lambda h: None):
     lane = lax.broadcasted_iota(jnp.int32, (NSEL, HD), 1)
-    stats = jnp.zeros((NSEL, HD), F32)
+
+    def score(h):
+        ready(h)
+        return [nt(q_of(h), keys) for keys in keys_of(h)]
+
+    def finish(h, weights, top, stats):
+        both = sum(nn(p, with_ones(vals)) for p, vals in zip(weights, vals_of(h)))
+        out[:, head_cols(h)] = (both[:, :HD] / both[:, HD:]).astype(BF)
+        return jnp.where(lane % heads == h, top + jnp.log2(both[:, HD:]), stats)
+
+    stats, last, scores = jnp.zeros((NSEL, HD), F32), None, score(0)
     for h in range(heads):
-        keys = jnp.concatenate(keys_of(h), axis=0)
-        vals = jnp.concatenate(vals_of(h), axis=0)
-        o, m = softmax_parts([nt(q_of(h), keys)], [vals])
-        out[:, head_cols(h)] = o.astype(BF)
-        stats = jnp.where(lane % heads == h, m, stats)
+        ahead = score(h + 1) if h + 1 < heads else None
+        top = functools.reduce(jnp.maximum, [jnp.max(s, axis=1, keepdims=True) for s in scores]) * SCALE
+        weights = [jnp.exp2(s * SCALE - top).astype(BF) for s in scores]
+        if last is not None:
+            stats = finish(*last, stats)
+        last, scores = (h, weights, top), ahead
+    stats = finish(*last, stats)
     out[:, heads * HD :] = in_three(stats, lane, heads)
 
 
@@ -202,13 +214,21 @@
                             sems.at[len(copies)],
                         )
                     )
-        run_copies(copies)
+        for c in copies:
+            c.start()
+
+        def ready(h):
+            if h % GH == 0:
+                for c in copies[8 * (h // GH) : 8 * (h // GH) + 8]:
+                    c.wait()
+
         near_part(
             ASK * GH,
             lambda h: qr[:, head_cols(h)],
             lambda h: [keys[:, head_cols(h)]],
             lambda h: [vals[:, head_cols(h)]],
             out,
+            ready,
         )
 
 
@@ -598,7 +618,7 @@
         out_places=[HBM, VMEM],
     )
     near_here = hbm(near_here)
-    far_back, near_back, out = lax.optimization_barrier((far_back, near_back, out))
+    far_back, out = lax.optimization_barrier((far_back, out))
     far_back_other = move(far_back, CORE)
     return call(
         finish_kernel,

time: 66.9 us -> 65.8 us (0.984)
  the two profiles are of different devices: /device:TPU:97 before, /device:TPU:65 now
where the time goes in v2:
time: 65.8 us; the launch traced here: 64.8 us
  Pallas kernels  31.4 us (48%)
  starting transfers between devices  25.6 us (39%)
  waiting for transfers between devices  7.51 us (11%)
    pallas_call x7, Pallas kernels, call(): pl.pallas_call(kernel, out_shape=outs, in_specs=[SMEM] + places, out_spec...  31.4 us
    ppermute x10, starting transfers between devices, move(): return lax.ppermute(array, AXES, pairs)  10.9 us
    all_to_all x1, starting transfers between devices, device_part(): far_back = lax.all_to_all(far_out, ('x', 'y'), 0, 0, tiled=True)  7.97 us
    all_to_all x1, starting transfers between devices, device_part(): far_mine = lax.all_to_all(far_pack, ('x', 'y'), 0, 0, tiled=True)  6.75 us
    all_to_all x1, waiting for transfers between devices, device_part(): far_back = lax.all_to_all(far_out, ('x', 'y'), 0, 0, tiled=True)  4.64 us
    ppermute x10, waiting for transfers between devices, move(): return lax.ppermute(array, AXES, pairs)  2.86 us
  transfers between devices with their start and end apart: 12, of which 3 were waited for; matrix products, arithmetic and copies ran while one was open for 0% of the time, Pallas kernels for 39%

profile of v2, /device:TPU:65, one launch (start us, length us, event | category | flops | bytes accessed | tf_op | source)
XLA Modules:
  0.0 64.8 jit_solution(6207042779894552508)
XLA Ops:
  0.0 3.6 %pack_first.1 = (bf16[256,1536]{1,0:T(8,128)(2,1)}, bf16[4,3,64,512]{3,2,1,0:T(8,128)(2,1)S(1)}, bf16[4,3,64,512]{3,2,1,0:T(8,128)(2,1)S(1)}) custom-call(s32[2,4]{1,0:T(2,128)} %offsets.13, bf16[512,2048]{1,0:T(8,128)(2,1)} %q.3, bf16[512,2048]{1,0:T(8,128)(2,1)} %k.3, bf16[512,2048]{1,0:T(8,128)(2,1)} %v.3), custom_call_target="tpu_custom_call" | custom-call | flops 1000 | bytes 1000 | tf_op jit(solution)/shard_map/pack_first/pallas_call | solution.py:552
  3.6 0.8 %collective-permute-start.1 = (bf16[4,3,64,512]{3,2,1,0:T(8,128)(2,1)S(1)}, bf16[4,3,64,512]{3,2,1,0:T(8,128)(2,1)S(1)}, u32[]{:S(2)}, u32[]{:S(2)}) collective-permute-start(bf16[4,3,64,512]{3,2,1,0:T(8,128)(2,1)S(1)} %get-tuple-element.22), channel_id=1, source_target_pairs={{0,1},{1,0},{2,3},{3,2},{4,5},{5,4},{6,7},{7,6},{8,9},{9,8},{10,11... | collective-permute-start | bytes 2359304 | tf_op jit(solution)/shard_map/ppermute | solution.py:66
  4.4 0.1 collective-permute-start.3
  4.5 0.4 collective-permute-start.4
  4.9 1.6 %collective-permute-done.1.received = bf16[4,3,64,512]{3,2,1,0:T(8,128)(2,1)S(1)} collective-permute-done((bf16[4,3,64,512]{3,2,1,0:T(8,128)(2,1)S(1)}, bf16[4,3,64,512]{3,2,1,0:T(8,128)(2,1)S(1)}, u32[]{:S(2)}, u32[]{:S(2)}) %collective-permute-start.1) | collective-permute-done | bytes 786464 | tf_op jit(solution)/shard_map/ppermute | solution.py:66
  6.5 0.4 collective-permute-start.2
  6.9 1.4 %collective-permute-start = (bf16[256,1536]{1,0:T(8,128)(2,1)}, bf16[256,1536]{1,0:T(8,128)(2,1)}, u32[]{:S(2)}, u32[]{:S(2)}) collective-permute-start(bf16[256,1536]{1,0:T(8,128)(2,1)} %get-tuple-element.20), channel_id=1, source_target_pairs={{0,2},{1,3},{2,0},{3,1},{4,6},{5,7},{6,4},{7,5},{8,10},{9,11},{10,... | collective-permute-start | bytes 2359304 | tf_op jit(solution)/shard_map/ppermute | solution.py:66
  8.3 1.9 %pack_second.1 = bf16[16,3,64,128]{3,2,1,0:T(8,128)(2,1)} custom-call(s32[2,4]{1,0:T(2,128)} %offsets.13, bf16[4,3,64,512]{3,2,1,0:T(8,128)(2,1)S(1)} %get-tuple-element.21.kept, bf16[4,3,64,512]{3,2,1,0:T(8,128)(2,1)S(1)} %collective-permute-done.1.received), custom_call_target="tpu_custom_call" | custom-call | flops 1000 | bytes 1000 | tf_op jit(solution)/shard_map/pack_second/pallas_call | solution.py:552
  10.1 6.8 %all-to-all-start = ((bf16[16,3,64,128]{3,2,1,0:T(8,128)(2,1)}), bf16[16,3,64,128]{3,2,1,0:T(8,128)(2,1)S(1)}, u32[]{:S(2)}, u32[]{:S(2)}) async-start(bf16[16,3,64,128]{3,2,1,0:T(8,128)(2,1)} %pack_second.1), calls=%async_computation | async-start | bytes 1572864 | tf_op jit(solution)/shard_map/all_to_all | solution.py:579
  16.9 0.0 collective-permute-done.3.ko_in.ko
  16.9 0.0 collective-permute-done.2.qo_in
  16.9 11.7 %local_kernel.1 = (bf16[256,2176]{1,0:T(8,128)(2,1)S(1)}, bf16[256,2176]{1,0:T(8,128)(2,1)}) custom-call(s32[2,4]{1,0:T(2,128)} %offsets.13, bf16[512,2048]{1,0:T(8,128)(2,1)} %q.3, bf16[512,2048]{1,0:T(8,128)(2,1)} %collective-permute-done.2.qo_in, bf16[512,2048]{1,0:T(8,128)(2,1)} %k.3, bf16[512,2048]{1,0:T(8,128)(2,1)} %collective-permute-done.3.ko_in.ko, ...), custom_call_target="tpu_custom_call" | custom-call | flops 10000000000 | bytes 1000 | tf_op jit(solution)/shard_map/local_kernel/pallas_call | solution.py:552
  28.6 1.9 %collective-permute-start.5 = (bf16[256,2176]{1,0:T(8,128)(2,1)}, bf16[256,2176]{1,0:T(8,128)(2,1)S(1)}, u32[]{:S(2)}, u32[]{:S(2)}) collective-permute-start(bf16[256,2176]{1,0:T(8,128)(2,1)} %get-tuple-element.27), channel_id=1, source_target_pairs={{0,1},{1,0},{2,3},{3,2},{4,5},{5,4},{6,7},{7,6},{8,9},{9,8},{10,11... | collective-permute-start | bytes 3342344 | tf_op jit(solution)/shard_map/ppermute | solution.py:66
  30.5 1.9 %collective-permute-start.7 = (bf16[16,3,64,128]{3,2,1,0:T(8,128)(2,1)S(1)}, bf16[16,3,64,128]{3,2,1,0:T(8,128)(2,1)S(1)}, u32[]{:S(2)}, u32[]{:S(2)}) collective-permute-start(bf16[16,3,64,128]{3,2,1,0:T(8,128)(2,1)S(1)} %all-to-all-done.mine), channel_id=1, source_target_pairs={{0,1},{1,0},{2,3},{3,2},{4,5},{5,4},{6,7},{7,6},{8,9},{9,8},{10,11... | collective-permute-start | bytes 2359304 | tf_op jit(solution)/shard_map/ppermute | solution.py:66
  32.4 0.0 collective-permute-start.8
  32.4 6.2 %near_even.1 = bf16[256,1664]{1,0:T(8,128)(2,1)} custom-call(s32[2,4]{1,0:T(2,128)} %offsets.13, bf16[256,1536]{1,0:T(8,128)(2,1)} %collective-permute-done.qr.kv_a, bf16[512,2048]{1,0:T(8,128)(2,1)} %k.3, bf16[512,2048]{1,0:T(8,128)(2,1)} %collective-permute-done.3.ko_in.ko, bf16[512,2048]{1,0:T(8,128)(2,1)} %v.3, ...), custom_call_target="tpu_custom_call" | custom-call | flops 1000 | bytes 1000 | tf_op jit(solution)/shard_map/near_even/pallas_call | solution.py:552
  38.6 2.2 %collective-permute-start.6 = (bf16[256,1664]{1,0:T(8,128)(2,1)}, bf16[256,1664]{1,0:T(8,128)(2,1)}, u32[]{:S(2)}, u32[]{:S(2)}) collective-permute-start(bf16[256,1664]{1,0:T(8,128)(2,1)} %near_even.1), channel_id=1, source_target_pairs={{0,2},{1,3},{4,6},{5,7},{8,10},{9,11},{12,14},{13,15},{16,18},{17,... | collective-permute-start | bytes 2555912 | tf_op jit(solution)/shard_map/ppermute | solution.py:66
  40.8 1.6 %far_kernel.1 = bf16[16,80,128]{2,1,0:T(8,128)(2,1)} custom-call(s32[2,4]{1,0:T(2,128)} %offsets.13, bf16[16,3,64,128]{3,2,1,0:T(8,128)(2,1)S(1)} %all-to-all-done.mine, bf16[16,3,64,128]{3,2,1,0:T(8,128)(2,1)S(1)} %collective-permute-done.7.other), custom_call_target="tpu_custom_call" | custom-call | flops 1000 | bytes 1000 | tf_op jit(solution)/shard_map/far_kernel/pallas_call | solution.py:552
  42.5 8.0 %all-to-all-start.1 = ((bf16[16,80,128]{2,1,0:T(8,128)(2,1)}), bf16[16,80,128]{2,1,0:T(8,128)(2,1)S(1)}, u32[]{:S(2)}, u32[]{:S(2)}) async-start(bf16[16,80,128]{2,1,0:T(8,128)(2,1)} %far_kernel.1), calls=%async_computation.1 | async-start | bytes 655360 | tf_op jit(solution)/shard_map/all_to_all | solution.py:606
  50.5 3.6 %settle.1 = (bf16[512,2048]{1,0:T(8,128)(2,1)}, bf16[256,640]{1,0:T(8,128)(2,1)}) custom-call(s32[2,4]{1,0:T(2,128)} %offsets.13, bf16[512,2048]{1,0:T(8,128)(2,1)} %q.3, bf16[256,1536]{1,0:T(8,128)(2,1)} %collective-permute-done.qr.kv_a, bf16[256,1536]{1,0:T(8,128)(2,1)} %collective-permute-done.8.kv_b, bf16[256,2176]{1,0:T(8,128)(2,1)S(1)} %get-tuple-element.26.mine, ...), custom_call_target="tpu_custom_call" | custom-call | flops 1000 | bytes 1000 | tf_op jit(solution)/shard_map/settle/pallas_call | solution.py:552
  54.1 4.6 %all-to-all-done.1.far_own = bf16[16,80,128]{2,1,0:T(8,128)(2,1)S(1)} async-done(((bf16[16,80,128]{2,1,0:T(8,128)(2,1)}), bf16[16,80,128]{2,1,0:T(8,128)(2,1)S(1)}, u32[]{:S(2)}, u32[]{:S(2)}) %all-to-all-start.1) | async-done | bytes 327712 | tf_op jit(solution)/shard_map/all_to_all | solution.py:606
  58.7 1.8 %collective-permute-start.9 = (bf16[16,80,128]{2,1,0:T(8,128)(2,1)S(1)}, bf16[16,80,128]{2,1,0:T(8,128)(2,1)S(1)}, u32[]{:S(2)}, u32[]{:S(2)}) collective-permute-start(bf16[16,80,128]{2,1,0:T(8,128)(2,1)S(1)} %all-to-all-done.1.far_own), channel_id=1, source_target_pairs={{0,1},{1,0},{2,3},{3,2},{4,5},{5,4},{6,7},{7,6},{8,9},{9,8},{10,11... | collective-permute-start | bytes 983048 | tf_op jit(solution)/shard_map/ppermute | solution.py:66
  60.6 1.3 %collective-permute-done.9.far_oth = bf16[16,80,128]{2,1,0:T(8,128)(2,1)S(1)} collective-permute-done((bf16[16,80,128]{2,1,0:T(8,128)(2,1)S(1)}, bf16[16,80,128]{2,1,0:T(8,128)(2,1)S(1)}, u32[]{:S(2)}, u32[]{:S(2)}) %collective-permute-start.9) | collective-permute-done | bytes 327712 | tf_op jit(solution)/shard_map/ppermute | solution.py:66
  61.8 2.8 %finish_kernel.1 = bf16[512,2048]{1,0:T(8,128)(2,1)} custom-call(s32[2,4]{1,0:T(2,128)} %offsets.13, bf16[256,2176]{1,0:T(8,128)(2,1)S(1)} %get-tuple-element.26.mine, bf16[256,2176]{1,0:T(8,128)(2,1)S(1)} %collective-permute-done.5.back, bf16[256,1664]{1,0:T(8,128)(2,1)} %collective-permute-done.6.near_a, ...), custom_call_target="tpu_custom_call", output_to_operand_aliasing={{}: (7, {})} | custom-call | flops 1000 | bytes 1000 | tf_op jit(solution)/shard_map/finish_kernel/pallas_call | solution.py:552
  (9 shorter events, 0.0 us)
Async XLA Ops:
  0.0 6.5 %copy-start = (bf16[512,2048]{1,0:T(8,128)(2,1)S(1)}, bf16[512,2048]{1,0:T(8,128)(2,1)}, u32[]{:S(2)}) copy-start(bf16[512,2048]{1,0:T(8,128)(2,1)} %q.3) | copy-start | bytes 6291460
  3.6 2.9 %collective-permute-start.1 = (bf16[4,3,64,512]{3,2,1,0:T(8,128)(2,1)S(1)}, bf16[4,3,64,512]{3,2,1,0:T(8,128)(2,1)S(1)}, u32[]{:S(2)}, u32[]{:S(2)}) collective-permute-start(bf16[4,3,64,512]{3,2,1,0:T(8,128)(2,1)S(1)} %get-tuple-element.22), channel_id=1, source_target_pairs={{0,1},{1,0},{2,3},{3,2},{4,5},{5,4},{6,7},{7,6},{8,9},{9,8},{10,11... | collective-permute-start | bytes 2359304 | tf_op jit(solution)/shard_map/ppermute | solution.py:66
  4.4 12.5 %collective-permute-start.3 = (bf16[512,2048]{1,0:T(8,128)(2,1)}, bf16[512,2048]{1,0:T(8,128)(2,1)}, u32[]{:S(2)}, u32[]{:S(2)}) collective-permute-start(bf16[512,2048]{1,0:T(8,128)(2,1)} %k.3), channel_id=1, source_target_pairs={{0,1},{1,0},{2,3},{3,2},{4,5},{5,4},{6,7},{7,6},{8,9},{9,8},{10,11... | collective-permute-start | bytes 6291464 | tf_op jit(solution)/shard_map/ppermute | solution.py:66
  4.5 12.4 %collective-permute-start.4 = (bf16[512,2048]{1,0:T(8,128)(2,1)}, bf16[512,2048]{1,0:T(8,128)(2,1)}, u32[]{:S(2)}, u32[]{:S(2)}) collective-permute-start(bf16[512,2048]{1,0:T(8,128)(2,1)} %v.3), channel_id=1, source_target_pairs={{0,1},{1,0},{2,3},{3,2},{4,5},{5,4},{6,7},{7,6},{8,9},{9,8},{10,11... | collective-permute-start | bytes 6291464 | tf_op jit(solution)/shard_map/ppermute | solution.py:66
  6.5 10.4 %collective-permute-start.2 = (bf16[512,2048]{1,0:T(8,128)(2,1)S(1)}, bf16[512,2048]{1,0:T(8,128)(2,1)}, u32[]{:S(2)}, u32[]{:S(2)}) collective-permute-start(bf16[512,2048]{1,0:T(8,128)(2,1)S(1)} %copy-done), channel_id=1, source_target_pairs={{0,1},{1,0},{2,3},{3,2},{4,5},{5,4},{6,7},{7,6},{8,9},{9,8},{10,11... | collective-permute-start | bytes 6291464 | tf_op jit(solution)/shard_map/ppermute | solution.py:66
  6.9 23.6 %collective-permute-start = (bf16[256,1536]{1,0:T(8,128)(2,1)}, bf16[256,1536]{1,0:T(8,128)(2,1)}, u32[]{:S(2)}, u32[]{:S(2)}) collective-permute-start(bf16[256,1536]{1,0:T(8,128)(2,1)} %get-tuple-element.20), channel_id=1, source_target_pairs={{0,2},{1,3},{2,0},{3,1},{4,6},{5,7},{6,4},{7,5},{8,10},{9,11},{10,... | collective-permute-start | bytes 2359304 | tf_op jit(solution)/shard_map/ppermute | solution.py:66
  10.1 20.3 %all-to-all-start = ((bf16[16,3,64,128]{3,2,1,0:T(8,128)(2,1)}), bf16[16,3,64,128]{3,2,1,0:T(8,128)(2,1)S(1)}, u32[]{:S(2)}, u32[]{:S(2)}) async-start(bf16[16,3,64,128]{3,2,1,0:T(8,128)(2,1)} %pack_second.1), calls=%async_computation | async-start | bytes 1572864 | tf_op jit(solution)/shard_map/all_to_all | solution.py:579
  28.6 21.8 %collective-permute-start.5 = (bf16[256,2176]{1,0:T(8,128)(2,1)}, bf16[256,2176]{1,0:T(8,128)(2,1)S(1)}, u32[]{:S(2)}, u32[]{:S(2)}) collective-permute-start(bf16[256,2176]{1,0:T(8,128)(2,1)} %get-tuple-element.27), channel_id=1, source_target_pairs={{0,1},{1,0},{2,3},{3,2},{4,5},{5,4},{6,7},{7,6},{8,9},{9,8},{10,11... | collective-permute-start | bytes 3342344 | tf_op jit(solution)/shard_map/ppermute | solution.py:66
  30.5 10.3 %collective-permute-start.7 = (bf16[16,3,64,128]{3,2,1,0:T(8,128)(2,1)S(1)}, bf16[16,3,64,128]{3,2,1,0:T(8,128)(2,1)S(1)}, u32[]{:S(2)}, u32[]{:S(2)}) collective-permute-start(bf16[16,3,64,128]{3,2,1,0:T(8,128)(2,1)S(1)} %all-to-all-done.mine), channel_id=1, source_target_pairs={{0,1},{1,0},{2,3},{3,2},{4,5},{5,4},{6,7},{7,6},{8,9},{9,8},{10,11... | collective-permute-start | bytes 2359304 | tf_op jit(solution)/shard_map/ppermute | solution.py:66
  32.4 18.1 %collective-permute-start.8 = (bf16[256,1536]{1,0:T(8,128)(2,1)}, bf16[256,1536]{1,0:T(8,128)(2,1)}, u32[]{:S(2)}, u32[]{:S(2)}) collective-permute-start(bf16[256,1536]{1,0:T(8,128)(2,1)} %collective-permute-done.qr.kv_a), channel_id=1, source_target_pairs={{0,1},{1,0},{2,3},{3,2},{4,5},{5,4},{6,7},{7,6},{8,9},{9,8},{10,11... | collective-permute-start | bytes 2359304 | tf_op jit(solution)/shard_map/ppermute | solution.py:66
  38.6 21.9 %collective-permute-start.6 = (bf16[256,1664]{1,0:T(8,128)(2,1)}, bf16[256,1664]{1,0:T(8,128)(2,1)}, u32[]{:S(2)}, u32[]{:S(2)}) collective-permute-start(bf16[256,1664]{1,0:T(8,128)(2,1)} %near_even.1), channel_id=1, source_target_pairs={{0,2},{1,3},{4,6},{5,7},{8,10},{9,11},{12,14},{13,15},{16,18},{17,... | collective-permute-start | bytes 2555912 | tf_op jit(solution)/shard_map/ppermute | solution.py:66
  42.5 16.2 %all-to-all-start.1 = ((bf16[16,80,128]{2,1,0:T(8,128)(2,1)}), bf16[16,80,128]{2,1,0:T(8,128)(2,1)S(1)}, u32[]{:S(2)}, u32[]{:S(2)}) async-start(bf16[16,80,128]{2,1,0:T(8,128)(2,1)} %far_kernel.1), calls=%async_computation.1 | async-start | bytes 655360 | tf_op jit(solution)/shard_map/all_to_all | solution.py:606
  58.7 3.1 %collective-permute-start.9 = (bf16[16,80,128]{2,1,0:T(8,128)(2,1)S(1)}, bf16[16,80,128]{2,1,0:T(8,128)(2,1)S(1)}, u32[]{:S(2)}, u32[]{:S(2)}) collective-permute-start(bf16[16,80,128]{2,1,0:T(8,128)(2,1)S(1)} %all-to-all-done.1.far_own), channel_id=1, source_target_pairs={{0,1},{1,0},{2,3},{3,2},{4,5},{5,4},{6,7},{7,6},{8,9},{9,8},{10,11... | collective-permute-start | bytes 983048 | tf_op jit(solution)/shard_map/ppermute | solution.py:66

commit v3 on v2

--- a/solution.py
+++ b/solution.py
@@ -173,7 +173,7 @@
     return slice(h * HD, (h + 1) * HD)
 
 
-def near_part(heads, q_of, keys_of, vals_of, out, ready=lambda h: None):
+def near_part(heads, q_of, keys_of, vals_of, out, ready=lambda h: None, left=lambda h: None):
     lane = lax.broadcasted_iota(jnp.int32, (NSEL, HD), 1)
 
     def score(h):
@@ -183,6 +183,7 @@
     def finish(h, weights, top, stats):
         both = sum(nn(p, with_ones(vals)) for p, vals in zip(weights, vals_of(h)))
         out[:, head_cols(h)] = (both[:, :HD] / both[:, HD:]).astype(BF)
+        left(h)
         return jnp.where(lane % heads == h, top + jnp.log2(both[:, HD:]), stats)
 
     stats, last, scores = jnp.zeros((NSEL, HD), F32), None, score(0)
@@ -197,39 +198,51 @@
     out[:, heads * HD :] = in_three(stats, lane, heads)
 
 
-def near_even(offsets, qr, k, ko, v, vo, out, keys, vals, sems):
+def near_even(offsets, qr_in, k, ko, v, vo, out, keys, vals, qr, done, sems, out_sems):
     here = Place(offsets)
 
     @pl.when(jnp.logical_not(here.odd))
     def _():
         copies = []
         for g in range(ASK):
+            pieces = [(qr_in.at[:, group_cols(g)], qr.at[:, group_cols(g)])]
             for n, (source, half) in enumerate([(0, 0), (0, 1), (1, 0), (1, 1)]):
                 rows = rows_at((here.near(g) + 2 * half) * BLK, BLK)
                 for two, target in (((k, ko), keys), ((v, vo), vals)):
-                    copies.append(
-                        pltpu.make_async_copy(
-                            two[source].at[rows, group_cols(g)],
-                            target.at[pl.ds(n * BLK, BLK), group_cols(g)],
-                            sems.at[len(copies)],
-                        )
+                    pieces.append(
+                        (two[source].at[rows, group_cols(g)], target.at[pl.ds(n * BLK, BLK), group_cols(g)])
                     )
-        for c in copies:
+            copies.append(
+                [pltpu.make_async_copy(x, y, sems.at[g, i]) for i, (x, y) in enumerate(pieces)]
+            )
+        for c in sum(copies, []):
             c.start()
 
         def ready(h):
             if h % GH == 0:
-                for c in copies[8 * (h // GH) : 8 * (h // GH) + 8]:
+                for c in copies[h // GH]:
                     c.wait()
+
+        def leave(g):
+            cols = group_cols(g) if g < ASK else pl.ds(ASK * GW, HD)
+            return pltpu.make_async_copy(done.at[:, cols], out.at[:, cols], out_sems.at[g])
+
+        def left(h):
+            if h % GH == GH - 1:
+                leave(h // GH).start()
 
         near_part(
             ASK * GH,
             lambda h: qr[:, head_cols(h)],
             lambda h: [keys[:, head_cols(h)]],
             lambda h: [vals[:, head_cols(h)]],
-            out,
+            done,
             ready,
+            left,
         )
+        leave(ASK).start()
+        for g in range(ASK + 1):
+            leave(g).wait()
 
 
 def far_kernel(offsets, mine, other, out):
@@ -467,10 +480,21 @@
 
 
 def finish_kernel(
-    offsets, mine, back, near_a, far_own, far_oth, near_in, before, out, near_o, far_o, near_b, near_sems, far_sems, sem
+    offsets, mine, back, far_own, far_oth, ask_in, near_in, before, out, *rest
 ):
     here = Place(offsets)
+    near_o, far_o, near_a, near_b, near_sems, far_sems, ask_sems, sem = rest
     nears, halves = (near_a, near_b), (mine, back)
+
+    def ask_copy(g):
+        cols = group_cols(g) if g < ASK else pl.ds(ASK * GW, HD)
+        return pltpu.make_async_copy(ask_in.at[:, cols], near_a.at[:, cols], ask_sems.at[g])
+
+    @pl.when(here.odd)
+    def _():
+        for g in (ASK, *range(ASK)):
+            ask_copy(g).start()
+
     want_near_b = here.odd & here.far_here(ASK)
     fetch = pltpu.make_async_copy(near_in, near_b, sem)
 
@@ -491,6 +515,13 @@
 
     for g in range(ASK):
         rows = rows_at(here.near(g) * BLK, BLK)
+
+        @pl.when(here.odd)
+        def _():
+            if g == 0:
+                ask_copy(ASK).wait()
+            ask_copy(g).wait()
+
         for half in range(2):
 
             @pl.when(near_here(g, half))
@@ -594,11 +625,17 @@
     far_other, near_ro = move(far_mine, CORE), move(near_r, CORE)
     near_out = call(
         near_even,
-        shape(NSEL, ASK * GW + HD),
-        (near_r, kh, ko, vh, vo),
-        [VMEM] + [HBM] * 4,
-        sems=8 * ASK,
-        scratch=[pltpu.VMEM((ROWS, ASK * GW), BF)] * 2,
+        pltpu.HBM((NSEL, ASK * GW + HD), BF),
+        (hbm(near_r), kh, ko, vh, vo),
+        [HBM] * 5,
+        scratch=[pltpu.VMEM((ROWS, ASK * GW), BF)] * 2
+        + [
+            pltpu.VMEM((NSEL, ASK * GW), BF),
+            pltpu.VMEM((NSEL, ASK * GW + HD), BF),
+            pltpu.SemaphoreType.DMA((ASK, 9)),
+            pltpu.SemaphoreType.DMA((ASK + 1,)),
+        ],
+        out_places=HBM,
     )
     near_back = move(near_out, TO_ODD)
     far_other, near_out = lax.optimization_barrier((far_other, near_out))
@@ -623,14 +660,16 @@
     return call(
         finish_kernel,
         shape(ROWS, HEADS * HD),
-        (mine, back, near_back, far_back, far_back_other, near_here, out),
-        [VMEM] * 5 + [HBM] * 2,
+        (mine, back, far_back, far_back_other, hbm(near_back), near_here, out),
+        [VMEM] * 4 + [HBM] * 3,
         scratch=[
             pltpu.VMEM((ASK, 2, BLK, GW), BF),
             pltpu.VMEM((GROUPS, BLK, GW), BF),
+            pltpu.VMEM((NSEL, ASK * GW + HD), BF),
             pltpu.VMEM((NSEL, GW + HD), BF),
             pltpu.SemaphoreType.DMA((ASK, 2)),
             pltpu.SemaphoreType.DMA((GROUPS,)),
+            pltpu.SemaphoreType.DMA((ASK + 1,)),
             pltpu.SemaphoreType.DMA,
         ],
         out_places=HBM,

time: 65.8 us -> 64.6 us (0.982)
  the two profiles are of different devices: /device:TPU:65 before, /device:TPU:96 now
where the time goes in v3:
time: 64.6 us; the launch traced here: 64.5 us
  Pallas kernels  31.7 us (49%)
  starting transfers between devices  19.4 us (30%)
  waiting for transfers between devices  13.1 us (20%)
    pallas_call x7, Pallas kernels, call(): pl.pallas_call(kernel, out_shape=outs, in_specs=[SMEM] + places, out_spec...  31.7 us
    all_to_all x1, starting transfers between devices, device_part(): far_back = lax.all_to_all(far_out, ('x', 'y'), 0, 0, tiled=True)  9.29 us
    ppermute x10, waiting for transfers between devices, move(): return lax.ppermute(array, AXES, pairs)  7.11 us
    all_to_all x1, starting transfers between devices, device_part(): far_mine = lax.all_to_all(far_pack, ('x', 'y'), 0, 0, tiled=True)  7.03 us
    all_to_all x1, waiting for transfers between devices, device_part(): far_back = lax.all_to_all(far_out, ('x', 'y'), 0, 0, tiled=True)  4.12 us
    ppermute x10, starting transfers between devices, move(): return lax.ppermute(array, AXES, pairs)  3.04 us
    all_to_all x1, waiting for transfers between devices, device_part(): far_mine = lax.all_to_all(far_pack, ('x', 'y'), 0, 0, tiled=True)  1.87 us
  transfers between devices with their start and end apart: 12, of which 5 were waited for; matrix products, arithmetic and copies ran while one was open for 0% of the time, Pallas kernels for 35%

profile of v3, /device:TPU:96, one launch (start us, length us, event | category | flops | bytes accessed | tf_op | source)
XLA Modules:
  0.0 64.5 jit_solution(9070495349580945865)
XLA Ops:
  0.0 3.7 %pack_first.1 = (bf16[256,1536]{1,0:T(8,128)(2,1)}, bf16[4,3,64,512]{3,2,1,0:T(8,128)(2,1)S(1)}, bf16[4,3,64,512]{3,2,1,0:T(8,128)(2,1)S(1)}) custom-call(s32[2,4]{1,0:T(2,128)} %offsets.13, bf16[512,2048]{1,0:T(8,128)(2,1)} %q.3, bf16[512,2048]{1,0:T(8,128)(2,1)} %k.3, bf16[512,2048]{1,0:T(8,128)(2,1)} %v.3), custom_call_target="tpu_custom_call" | custom-call | flops 1000 | bytes 1000 | tf_op jit(solution)/shard_map/pack_first/pallas_call | solution.py:583
  3.7 0.1 collective-permute-start.1
  3.8 0.5 collective-permute-start.3
  4.3 0.1 collective-permute-start.4
  4.4 1.9 %collective-permute-done.1.received = bf16[4,3,64,512]{3,2,1,0:T(8,128)(2,1)S(1)} collective-permute-done((bf16[4,3,64,512]{3,2,1,0:T(8,128)(2,1)S(1)}, bf16[4,3,64,512]{3,2,1,0:T(8,128)(2,1)S(1)}, u32[]{:S(2)}, u32[]{:S(2)}) %collective-permute-start.1) | collective-permute-done | bytes 786464 | tf_op jit(solution)/shard_map/ppermute | solution.py:66
  6.3 0.1 collective-permute-start.2
  6.4 0.3 collective-permute-start
  6.7 1.9 %pack_second.1 = bf16[16,3,64,128]{3,2,1,0:T(8,128)(2,1)} custom-call(s32[2,4]{1,0:T(2,128)} %offsets.13, bf16[4,3,64,512]{3,2,1,0:T(8,128)(2,1)S(1)} %get-tuple-element.21.kept, bf16[4,3,64,512]{3,2,1,0:T(8,128)(2,1)S(1)} %collective-permute-done.1.received), custom_call_target="tpu_custom_call" | custom-call | flops 1000 | bytes 1000 | tf_op jit(solution)/shard_map/pack_second/pallas_call | solution.py:583
  8.6 7.0 %all-to-all-start = ((bf16[16,3,64,128]{3,2,1,0:T(8,128)(2,1)}), bf16[16,3,64,128]{3,2,1,0:T(8,128)(2,1)S(1)}, u32[]{:S(2)}, u32[]{:S(2)}) async-start(bf16[16,3,64,128]{3,2,1,0:T(8,128)(2,1)} %pack_second.1), calls=%async_computation | async-start | bytes 1572864 | tf_op jit(solution)/shard_map/all_to_all | solution.py:610
  15.6 0.0 collective-permute-done.4.vo_in.vo
  15.7 0.0 collective-permute-done.2.qo_in
  15.7 12.7 %local_kernel.1 = (bf16[256,2176]{1,0:T(8,128)(2,1)S(1)}, bf16[256,2176]{1,0:T(8,128)(2,1)}) custom-call(s32[2,4]{1,0:T(2,128)} %offsets.13, bf16[512,2048]{1,0:T(8,128)(2,1)} %q.3, bf16[512,2048]{1,0:T(8,128)(2,1)} %collective-permute-done.2.qo_in, bf16[512,2048]{1,0:T(8,128)(2,1)} %k.3, bf16[512,2048]{1,0:T(8,128)(2,1)} %collective-permute-done.3.ko_in.ko, ...), custom_call_target="tpu_custom_call" | custom-call | flops 10000000000 | bytes 1000 | tf_op jit(solution)/shard_map/local_kernel/pallas_call | solution.py:583
  28.4 0.1 collective-permute-start.5
  28.5 1.9 %all-to-all-done.mine = bf16[16,3,64,128]{3,2,1,0:T(8,128)(2,1)S(1)} async-done(((bf16[16,3,64,128]{3,2,1,0:T(8,128)(2,1)}), bf16[16,3,64,128]{3,2,1,0:T(8,128)(2,1)S(1)}, u32[]{:S(2)}, u32[]{:S(2)}) %all-to-all-start) | async-done | bytes 786464 | tf_op jit(solution)/shard_map/all_to_all | solution.py:610
  30.4 0.5 collective-permute-start.7
  30.9 1.0 %near_even.1 = bf16[256,1664]{1,0:T(8,128)(2,1)} custom-call(s32[2,4]{1,0:T(2,128)} %offsets.13, bf16[256,1536]{1,0:T(8,128)(2,1)} %collective-permute-done.qr_in.kv_a, bf16[512,2048]{1,0:T(8,128)(2,1)} %k.3, bf16[512,2048]{1,0:T(8,128)(2,1)} %collective-permute-done.3.ko_in.ko, bf16[512,2048]{1,0:T(8,128)(2,1)} %v.3, ...), custom_call_target="tpu_custom_call" | custom-call | flops 1000 | bytes 1000 | tf_op jit(solution)/shard_map/near_even/pallas_call | solution.py:583
  31.9 1.3 %collective-permute-start.9 = (bf16[256,1664]{1,0:T(8,128)(2,1)}, bf16[256,1664]{1,0:T(8,128)(2,1)}, u32[]{:S(2)}, u32[]{:S(2)}) collective-permute-start(bf16[256,1664]{1,0:T(8,128)(2,1)} %near_even.1), channel_id=1, source_target_pairs={{0,2},{1,3},{4,6},{5,7},{8,10},{9,11},{12,14},{13,15},{16,18},{17,... | collective-permute-start | bytes 2555912 | tf_op jit(solution)/shard_map/ppermute | solution.py:66
  33.2 0.6 collective-permute-done.6.other
  33.8 1.6 %far_kernel.1 = bf16[16,80,128]{2,1,0:T(8,128)(2,1)} custom-call(s32[2,4]{1,0:T(2,128)} %offsets.13, bf16[16,3,64,128]{3,2,1,0:T(8,128)(2,1)S(1)} %all-to-all-done.mine, bf16[16,3,64,128]{3,2,1,0:T(8,128)(2,1)S(1)} %collective-permute-done.6.other), custom_call_target="tpu_custom_call" | custom-call | flops 1000 | bytes 1000 | tf_op jit(solution)/shard_map/far_kernel/pallas_call | solution.py:583
  35.4 9.3 %all-to-all-start.1 = ((bf16[16,80,128]{2,1,0:T(8,128)(2,1)}), bf16[16,80,128]{2,1,0:T(8,128)(2,1)S(1)}, u32[]{:S(2)}, u32[]{:S(2)}) async-start(bf16[16,80,128]{2,1,0:T(8,128)(2,1)} %far_kernel.1), calls=%async_computation.1 | async-start | bytes 655360 | tf_op jit(solution)/shard_map/all_to_all | solution.py:643
  44.7 5.5 %settle.1 = (bf16[512,2048]{1,0:T(8,128)(2,1)}, bf16[256,640]{1,0:T(8,128)(2,1)}) custom-call(s32[2,4]{1,0:T(2,128)} %offsets.13, bf16[512,2048]{1,0:T(8,128)(2,1)} %q.3, bf16[256,1536]{1,0:T(8,128)(2,1)} %collective-permute-done.qr_in.kv_a, bf16[256,1536]{1,0:T(8,128)(2,1)} %collective-permute-done.7.kv_b, bf16[256,2176]{1,0:T(8,128)(2,1)S(1)} %get-tuple-element.26.mine, ...), custom_call_target="tpu_custom_call" | custom-call | flops 1000 | bytes 1000 | tf_op jit(solution)/shard_map/settle/pallas_call | solution.py:583
  50.3 4.1 %all-to-all-done.1.far_own = bf16[16,80,128]{2,1,0:T(8,128)(2,1)S(1)} async-done(((bf16[16,80,128]{2,1,0:T(8,128)(2,1)}), bf16[16,80,128]{2,1,0:T(8,128)(2,1)S(1)}, u32[]{:S(2)}, u32[]{:S(2)}) %all-to-all-start.1) | async-done | bytes 327712 | tf_op jit(solution)/shard_map/all_to_all | solution.py:643
  54.4 4.6 %collective-permute-done.9.ask_in = bf16[256,1664]{1,0:T(8,128)(2,1)} collective-permute-done((bf16[256,1664]{1,0:T(8,128)(2,1)}, bf16[256,1664]{1,0:T(8,128)(2,1)}, u32[]{:S(2)}, u32[]{:S(2)}) %collective-permute-start.9) | collective-permute-done | bytes 852000 | tf_op jit(solution)/shard_map/ppermute | solution.py:66
  59.0 5.3 %finish_kernel.1 = bf16[512,2048]{1,0:T(8,128)(2,1)} custom-call(s32[2,4]{1,0:T(2,128)} %offsets.13, bf16[256,2176]{1,0:T(8,128)(2,1)S(1)} %get-tuple-element.26.mine, bf16[256,2176]{1,0:T(8,128)(2,1)S(1)} %collective-permute-done.5.back, bf16[16,80,128]{2,1,0:T(8,128)(2,1)S(1)} %all-to-all-done.1.far_own, ...), custom_call_target="tpu_custom_call", output_to_operand_aliasing={{}: (7, {})} | custom-call | flops 1000 | bytes 1000 | tf_op jit(solution)/shard_map/finish_kernel/pallas_call | solution.py:583
  (9 shorter events, 0.0 us)
Async XLA Ops:
  0.0 6.3 %copy-start = (bf16[512,2048]{1,0:T(8,128)(2,1)S(1)}, bf16[512,2048]{1,0:T(8,128)(2,1)}, u32[]{:S(2)}) copy-start(bf16[512,2048]{1,0:T(8,128)(2,1)} %q.3) | copy-start | bytes 6291460
  3.7 2.6 %collective-permute-start.1 = (bf16[4,3,64,512]{3,2,1,0:T(8,128)(2,1)S(1)}, bf16[4,3,64,512]{3,2,1,0:T(8,128)(2,1)S(1)}, u32[]{:S(2)}, u32[]{:S(2)}) collective-permute-start(bf16[4,3,64,512]{3,2,1,0:T(8,128)(2,1)S(1)} %get-tuple-element.22), channel_id=1, source_target_pairs={{0,1},{1,0},{2,3},{3,2},{4,5},{5,4},{6,7},{7,6},{8,9},{9,8},{10,11... | collective-permute-start | bytes 2359304 | tf_op jit(solution)/shard_map/ppermute | solution.py:66
  3.8 11.8 %collective-permute-start.3 = (bf16[512,2048]{1,0:T(8,128)(2,1)}, bf16[512,2048]{1,0:T(8,128)(2,1)}, u32[]{:S(2)}, u32[]{:S(2)}) collective-permute-start(bf16[512,2048]{1,0:T(8,128)(2,1)} %k.3), channel_id=1, source_target_pairs={{0,1},{1,0},{2,3},{3,2},{4,5},{5,4},{6,7},{7,6},{8,9},{9,8},{10,11... | collective-permute-start | bytes 6291464 | tf_op jit(solution)/shard_map/ppermute | solution.py:66
  4.3 11.4 %collective-permute-start.4 = (bf16[512,2048]{1,0:T(8,128)(2,1)}, bf16[512,2048]{1,0:T(8,128)(2,1)}, u32[]{:S(2)}, u32[]{:S(2)}) collective-permute-start(bf16[512,2048]{1,0:T(8,128)(2,1)} %v.3), channel_id=1, source_target_pairs={{0,1},{1,0},{2,3},{3,2},{4,5},{5,4},{6,7},{7,6},{8,9},{9,8},{10,11... | collective-permute-start | bytes 6291464 | tf_op jit(solution)/shard_map/ppermute | solution.py:66
  6.3 9.4 %collective-permute-start.2 = (bf16[512,2048]{1,0:T(8,128)(2,1)S(1)}, bf16[512,2048]{1,0:T(8,128)(2,1)}, u32[]{:S(2)}, u32[]{:S(2)}) collective-permute-start(bf16[512,2048]{1,0:T(8,128)(2,1)S(1)} %copy-done), channel_id=1, source_target_pairs={{0,1},{1,0},{2,3},{3,2},{4,5},{5,4},{6,7},{7,6},{8,9},{9,8},{10,11... | collective-permute-start | bytes 6291464 | tf_op jit(solution)/shard_map/ppermute | solution.py:66
  6.4 22.1 %collective-permute-start = (bf16[256,1536]{1,0:T(8,128)(2,1)}, bf16[256,1536]{1,0:T(8,128)(2,1)}, u32[]{:S(2)}, u32[]{:S(2)}) collective-permute-start(bf16[256,1536]{1,0:T(8,128)(2,1)} %get-tuple-element.20), channel_id=1, source_target_pairs={{0,2},{1,3},{2,0},{3,1},{4,6},{5,7},{6,4},{7,5},{8,10},{9,11},{10,... | collective-permute-start | bytes 2359304 | tf_op jit(solution)/shard_map/ppermute | solution.py:66
  8.6 21.8 %all-to-all-start = ((bf16[16,3,64,128]{3,2,1,0:T(8,128)(2,1)}), bf16[16,3,64,128]{3,2,1,0:T(8,128)(2,1)S(1)}, u32[]{:S(2)}, u32[]{:S(2)}) async-start(bf16[16,3,64,128]{3,2,1,0:T(8,128)(2,1)} %pack_second.1), calls=%async_computation | async-start | bytes 1572864 | tf_op jit(solution)/shard_map/all_to_all | solution.py:610
  28.4 16.3 %collective-permute-start.5 = (bf16[256,2176]{1,0:T(8,128)(2,1)}, bf16[256,2176]{1,0:T(8,128)(2,1)S(1)}, u32[]{:S(2)}, u32[]{:S(2)}) collective-permute-start(bf16[256,2176]{1,0:T(8,128)(2,1)} %get-tuple-element.27), channel_id=1, source_target_pairs={{0,1},{1,0},{2,3},{3,2},{4,5},{5,4},{6,7},{7,6},{8,9},{9,8},{10,11... | collective-permute-start | bytes 3342344 | tf_op jit(solution)/shard_map/ppermute | solution.py:66
  30.4 3.4 %collective-permute-start.6 = (bf16[16,3,64,128]{3,2,1,0:T(8,128)(2,1)S(1)}, bf16[16,3,64,128]{3,2,1,0:T(8,128)(2,1)S(1)}, u32[]{:S(2)}, u32[]{:S(2)}) collective-permute-start(bf16[16,3,64,128]{3,2,1,0:T(8,128)(2,1)S(1)} %all-to-all-done.mine), channel_id=1, source_target_pairs={{0,1},{1,0},{2,3},{3,2},{4,5},{5,4},{6,7},{7,6},{8,9},{9,8},{10,11... | collective-permute-start | bytes 2359304 | tf_op jit(solution)/shard_map/ppermute | solution.py:66
  30.4 14.3 %collective-permute-start.7 = (bf16[256,1536]{1,0:T(8,128)(2,1)}, bf16[256,1536]{1,0:T(8,128)(2,1)}, u32[]{:S(2)}, u32[]{:S(2)}) collective-permute-start(bf16[256,1536]{1,0:T(8,128)(2,1)} %collective-permute-done.qr_in.kv_a), channel_id=1, source_target_pairs={{0,1},{1,0},{2,3},{3,2},{4,5},{5,4},{6,7},{7,6},{8,9},{9,8},{10,11... | collective-permute-start | bytes 2359304 | tf_op jit(solution)/shard_map/ppermute | solution.py:66
  31.9 27.1 %collective-permute-start.9 = (bf16[256,1664]{1,0:T(8,128)(2,1)}, bf16[256,1664]{1,0:T(8,128)(2,1)}, u32[]{:S(2)}, u32[]{:S(2)}) collective-permute-start(bf16[256,1664]{1,0:T(8,128)(2,1)} %near_even.1), channel_id=1, source_target_pairs={{0,2},{1,3},{4,6},{5,7},{8,10},{9,11},{12,14},{13,15},{16,18},{17,... | collective-permute-start | bytes 2555912 | tf_op jit(solution)/shard_map/ppermute | solution.py:66
  35.4 19.0 %all-to-all-start.1 = ((bf16[16,80,128]{2,1,0:T(8,128)(2,1)}), bf16[16,80,128]{2,1,0:T(8,128)(2,1)S(1)}, u32[]{:S(2)}, u32[]{:S(2)}) async-start(bf16[16,80,128]{2,1,0:T(8,128)(2,1)} %far_kernel.1), calls=%async_computation.1 | async-start | bytes 655360 | tf_op jit(solution)/shard_map/all_to_all | solution.py:643
  54.4 4.6 %collective-permute-start.8 = (bf16[16,80,128]{2,1,0:T(8,128)(2,1)S(1)}, bf16[16,80,128]{2,1,0:T(8,128)(2,1)S(1)}, u32[]{:S(2)}, u32[]{:S(2)}) collective-permute-start(bf16[16,80,128]{2,1,0:T(8,128)(2,1)S(1)} %all-to-all-done.1.far_own), channel_id=1, source_target_pairs={{0,1},{1,0},{2,3},{3,2},{4,5},{5,4},{6,7},{7,6},{8,9},{9,8},{10,11... | collective-permute-start | bytes 983048 | tf_op jit(solution)/shard_map/ppermute | solution.py:66
